TPU v7x, 128 devices: a whole 4x4x4 slice. The times are simulated.
128 devices in a mesh: shard: 4 (over y_lo, core), replica: 32 (over z, x, y_hi).
Axes of the slice: x: 4, y: 4 (y_hi: 2, y_lo: 2; y = y_hi * 2 + y_lo), z: 4, core: 2. Of those that a mesh axis runs over, the one named last changes fastest.
Arguments:
- tokens: bfloat16 [128, 384, 960], P(('shard', 'replica')), may hold values from -6 to 6
- lengths: int32 [128, 4], P(('shard', 'replica')), may hold values from 0 to 384, as said below
- norm_attn: bfloat16 [960], P('shard'), may hold values from 0.5 to 1.5
- w_query: bfloat16 [960, 960], P('shard'), may hold values from -0.1875 to 0.1875
- w_key: bfloat16 [960, 320], P('shard'), may hold values from -0.1875 to 0.1875
- w_value: bfloat16 [960, 320], P('shard'), may hold values from -0.1875 to 0.1875
- w_out: bfloat16 [960, 960], P('shard'), may hold values from -2 to 2
- norm_mlp: bfloat16 [960], P('shard'), may hold values from 0.5 to 1.5
- w_gate: bfloat16 [960, 2560], P('shard'), may hold values from -0.1875 to 0.1875
- w_up: bfloat16 [960, 2560], P('shard'), may hold values from -0.1875 to 0.1875
- w_down: bfloat16 [2560, 960], P('shard'), may hold values from -0.125 to 0.125
- cotangent: bfloat16 [128, 384, 960], P(('shard', 'replica')), may hold values from -6 to 6
Outputs:
- out: bfloat16 [128, 384, 960], P(('shard', 'replica'))
- grad_in: float32 [128, 384, 960], P(('shard', 'replica'))
- grad_norm_attn: float32 [960], P('shard')
- grad_query: float32 [960, 960], P('shard')
- grad_key: float32 [960, 320], P('shard')
- grad_value: float32 [960, 320], P('shard')
- grad_out_proj: float32 [960, 960], P('shard')
- grad_norm_mlp: float32 [960], P('shard')
- grad_gate: float32 [960, 2560], P('shard')
- grad_up: float32 [960, 2560], P('shard')
- grad_down: float32 [2560, 960], P('shard')
Inputs may be any that keep to these rules, and one draw needn't show every extreme that they name: Row g lists the lengths of the sequences packed in order into pack g's 384 slots, zeros for unused entries; each row sums to 384.
All inputs are finite; a program needn't handle non-finite values.
Results may differ from a plain program's by a relative error of at most 0.028.
Values may be sent and summed in bfloat16 or wider, within the bound.
No kernel may reach another device: no remote copies, remote signals or barrier semaphores. Data moves between devices by JAX's collectives and lax.ppermute only.
A program may use at most 256 MiB of HBM per device.

v0:
```python
import jax
import jax.numpy as jnp
from jax import lax
from jax.experimental import pallas as pl
from jax.experimental.pallas import tpu as pltpu
from jax.sharding import Mesh
from jax.sharding import PartitionSpec as P

T = 384
D = 960
FF = 2560
HEADS = 15
KV = 5
GROUP = 3
HEAD_DIM = 64
BLOCK = 128
BLOCKS = T // BLOCK
STACK = GROUP * BLOCK
QK = (HEADS + KV) * HEAD_DIM
QKV = QK + KV * HEAD_DIM
PACK = 2 * QK
ROWS = D // 4
UNIT = 640
EVERY = ("y_lo", "core", "z", "x", "y_hi")
SHARD = ("y_lo", "core")
EPS = 1e-05
BASE = 100000.0
MASKED = -1e30
BF = jnp.bfloat16
F32 = jnp.float32
LIMIT = 52 * 2**20

ANY = pl.BlockSpec(memory_space=pl.ANY)
VMEM = pl.BlockSpec(memory_space=pltpu.VMEM)
SMEM = pl.BlockSpec(memory_space=pltpu.SMEM)


def shape(*dims, dtype=BF):
    return jax.ShapeDtypeStruct(dims, dtype)


def mult(left, right):
    return jnp.dot(left, right, preferred_element_type=F32)


def mult_tn(left, right):
    return lax.dot_general(left, right, (((0,), (0,)), ((), ())), preferred_element_type=F32)


def mult_nt(left, right):
    return lax.dot_general(left, right, (((1,), (1,)), ((), ())), preferred_element_type=F32)


def shard_at(me, flip, rows, unit):
    return pl.ds(pl.multiple_of(lax.bitwise_xor(me, jnp.int32(flip)) * rows, unit), rows)


def row_copies(pieces, full, me, sems, columns=None, at=0):
    copies = []
    for flip, source in enumerate(pieces):
        width = source.shape[1]
        target = pl.ds(at, width)
        if columns is not None:
            source, target = source.at[:, columns], pl.ds(at + columns.start, columns.size)
        copies.append(pltpu.make_async_copy(source, full.at[shard_at(me, flip, ROWS, 16), target], sems.at[flip]))
    return copies


def column_copies(pieces, full, me, sems):
    copies = []
    for k, (flip, start, size) in enumerate(((0, 0, D), (1, 0, D), (2, 0, D // 2), (2, D // 2, D // 2), (3, 0, D // 2), (3, D // 2, D // 2))):
        target = full.at[pl.ds(start, size), shard_at(me, flip, FF // 4, 128)]
        copies.append(pltpu.make_async_copy(pieces[k], target, sems.at[k]))
    return copies


def start_all(copies):
    for copy in copies:
        copy.start()


def wait_all(copies):
    for copy in copies:
        copy.wait()


def rope(u, cosine, sine, sign):
    lane = lax.broadcasted_iota(jnp.int32, u.shape, 1)
    turned = jnp.where(lane % HEAD_DIM < HEAD_DIM // 2, pltpu.roll(u, 96, 1), pltpu.roll(u, 32, 1))
    return u * cosine + sign * (turned * sine)


def rms_scale(v):
    return lax.rsqrt(jnp.mean(v * v, axis=-1, keepdims=True) + EPS)


def norm_back(v, gain, grad):
    scale = rms_scale(v)
    inner = grad * gain
    d_v = scale * inner - v * (scale * scale * scale) * jnp.mean(v * inner, axis=-1, keepdims=True)
    return d_v, jnp.sum(grad * v * scale, axis=0, keepdims=True)


def attention_kernel(me_ref, x_ref, gains_ref, cos_ref, sin_ref, start_ref, *refs):
    pieces, refs = refs[:8], refs[8:]
    (q_ref, k_ref, v_ref, p0_ref, p1_ref, p2_ref, x_out_ref, h_ref, b_ref, a_turned_ref, att_turned_ref, b_turned_ref, w, o, bias, att_ref, sems) = refs
    copies = row_copies(pieces[:4], w, me_ref[0], sems.at[0])
    copies += row_copies(pieces[4:], w, me_ref[0], sems.at[1], at=QK)
    start_all(copies)
    x_out_ref[...] = x_ref[...].T
    x = x_out_ref[...].astype(F32)
    a = (x * rms_scale(x) * gains_ref[0:1]).astype(BF)
    a_turned_ref[...] = a.T
    column = lax.broadcasted_iota(jnp.int32, (T, T), 1)
    row = lax.broadcasted_iota(jnp.int32, (T, T), 0)
    bias[...] = jnp.where((column >= start_ref[...]) & (column <= row), 0.0, MASKED)
    wait_all(copies)
    for c in range(QK // 256):
        wide = mult(a, w[:, 256 * c : 256 * (c + 1)])
        for half in range(2):
            u = rope(wide[:, 128 * half : 128 * half + 128], cos_ref[...], sin_ref[...], 1.0).astype(BF)
            for side in range(2):
                head = 4 * c + 2 * half + side
                one = u[:, HEAD_DIM * side : HEAD_DIM * (side + 1)]
                if head < HEADS:
                    for i in range(BLOCKS):
                        at = i * STACK + head % GROUP * BLOCK
                        q_ref[head // GROUP, at : at + BLOCK, :] = one[i * BLOCK : (i + 1) * BLOCK]
                else:
                    k_ref[head - HEADS] = one
    values = mult(a, w[:, QK + D :]).astype(BF)
    for j in range(KV):
        v_ref[j] = values[:, HEAD_DIM * j : HEAD_DIM * (j + 1)]
    probs = (p0_ref, p1_ref, p2_ref)

    def one_group(j, carry):
        for i in range(BLOCKS):
            keys = (i + 1) * BLOCK
            q = q_ref[j, i * STACK : (i + 1) * STACK, :]
            scores = mult_nt(q, k_ref[j, :keys, :]) * 0.125
            part = bias[i * BLOCK : (i + 1) * BLOCK, :keys]
            scores = scores + jnp.concatenate([part] * GROUP, axis=0)
            expo = jnp.exp(scores - jnp.max(scores, axis=-1, keepdims=True))
            prob = (expo * (1.0 / jnp.sum(expo, axis=-1, keepdims=True))).astype(BF)
            probs[i][j] = prob
            o[j, i * STACK : (i + 1) * STACK, :] = mult(prob, v_ref[j, :keys, :])
        return carry

    lax.fori_loop(0, KV, one_group, 0, unroll=True)
    for c in range(8):
        heads = [stacked_head(o, head) for head in range(2 * c, min(2 * c + 2, HEADS))]
        wide = jnp.concatenate(heads, axis=1) if len(heads) > 1 else heads[0]
        att_ref[:, 128 * c : 128 * c + wide.shape[1]] = wide.astype(BF)
    att = att_ref[...]
    att_turned_ref[...] = att.T
    h = x_out_ref[...].astype(F32) + mult(att, w[:, QK : QK + D])
    h_ref[...] = h
    b = (h * rms_scale(h) * gains_ref[1:2]).astype(BF)
    b_ref[...] = b
    b_turned_ref[...] = b.T


def stacked_head(ref, head):
    at = head % GROUP * BLOCK
    return jnp.concatenate(
        [ref[head // GROUP, i * STACK + at : i * STACK + at + BLOCK, :] for i in range(BLOCKS)], axis=0
    )


CHUNK = 512


def gate_kernel(me_ref, b_ref, *refs):
    pieces, (act_ref, silu_ref, slope_ref, w, sems) = refs[:8], refs[8:]
    chunks = FF // CHUNK
    copies = []
    for c in range(chunks):
        for k in range(2):
            part = pieces[4 * k : 4 * k + 4]
            copies.append(row_copies(part, w, me_ref[0], sems.at[2 * c + k], pl.ds(c * CHUNK, CHUNK), k * FF))
    for group in copies:
        start_all(group)
    b = b_ref[...]
    for c in range(chunks):
        at = c * CHUNK
        for group in copies[2 * c : 2 * c + 2]:
            wait_all(group)
        gate = mult(b, w[:, at : at + CHUNK])
        up = mult(b, w[:, FF + at : FF + at + CHUNK])
        sigma = jax.nn.sigmoid(gate)
        silu = gate * sigma
        act_ref[:, at : at + CHUNK] = (silu * up).astype(BF)
        silu_ref[:, at : at + CHUNK] = silu.astype(BF)
        slope_ref[:, at : at + CHUNK] = (up * sigma * (1.0 + gate * (1.0 - sigma))).astype(BF)


def mlp_kernel(me_ref, act_ref, silu_ref, slope_ref, h_ref, dy_ref, gains_ref, *refs):
    down, wide, refs = refs[:6], refs[6:14], refs[16:]
    (out_ref, d_gate_ref, d_up_ref, d_h_ref, d_low_ref, d_gain_ref, wd, w, sums, sems) = refs
    first = column_copies(down, wd, me_ref[0], sems.at[0])
    second = row_copies(wide[:4], w, me_ref[0], sems.at[1]) + row_copies(wide[4:], w, me_ref[0], sems.at[2], at=FF)
    start_all(first + second)
    wait_all(first)
    dy = dy_ref[...].T
    out_ref[...] = (h_ref[...] + mult_nt(act_ref[...], wd[...])).astype(BF)
    for c in range(FF // CHUNK):
        at = c * CHUNK
        d_act = mult(dy, wd[:, at : at + CHUNK])
        d_gate_ref[:, at : at + CHUNK] = (d_act * slope_ref[:, at : at + CHUNK].astype(F32)).astype(BF)
        d_up_ref[:, at : at + CHUNK] = (d_act * silu_ref[:, at : at + CHUNK].astype(F32)).astype(BF)
    wait_all(second)
    sums[...] = mult_nt(d_gate_ref[...], w[:, :FF]) + mult_nt(d_up_ref[...], w[:, FF:])
    d_norm, d_gain = norm_back(h_ref[...], gains_ref[1:2], sums[...])
    d_h = dy.astype(F32) + d_norm
    d_h_ref[...] = d_h
    d_low_ref[...] = d_h.astype(BF)
    d_gain_ref[...] = d_gain


def attention_back_kernel(me_ref, x_ref, gains_ref, cos_ref, sin_ref, d_low_ref, d_h_ref, q_ref, k_ref, v_ref, p0_ref, p1_ref, p2_ref, *refs):
    pieces, refs = refs[:8], refs[-9:]
    (d_qkv_ref, grad_ref, d_gain_ref, w, d_o, d_q, d_k, d_v, sems) = refs
    copies = row_copies(pieces[:4], w, me_ref[0], sems.at[0])
    copies += row_copies(pieces[4:], w, me_ref[0], sems.at[1], at=QK)
    start_all(copies)
    wait_all(copies)
    d_low = d_low_ref[...]
    for c in range(3):
        part = mult_nt(d_low, w[320 * c : 320 * (c + 1), QK : QK + D]).astype(BF)
        for side in range(5):
            head = 5 * c + side
            for i in range(BLOCKS):
                at = i * STACK + head % GROUP * BLOCK
                d_o[head // GROUP, at : at + BLOCK, :] = part[i * BLOCK : (i + 1) * BLOCK, HEAD_DIM * side : HEAD_DIM * (side + 1)]
    probs = (p0_ref, p1_ref, p2_ref)

    def one_group(j, carry):
        parts_k, parts_v = [], []
        for i in range(BLOCKS):
            keys = (i + 1) * BLOCK
            stack = slice(i * STACK, (i + 1) * STACK)
            low = probs[i][j]
            d_one = d_o[j, stack, :]
            prob = low.astype(F32)
            d_prob = mult_nt(d_one, v_ref[j, :keys, :])
            inner = jnp.sum(prob * d_prob, axis=-1, keepdims=True)
            d_scores = (prob * (d_prob - inner)).astype(BF)
            d_q[j, stack, :] = mult(d_scores, k_ref[j, :keys, :]) * 0.125
            parts_k.append(mult_tn(d_scores, q_ref[j, stack, :]))
            parts_v.append(mult_tn(low, d_one))
        for i in range(BLOCKS):
            rows = slice(i * BLOCK, (i + 1) * BLOCK)
            d_k[j, rows, :] = sum(part[rows] for part in parts_k[i:]) * 0.125
            d_v[j, rows, :] = sum(part[rows] for part in parts_v[i:])
        return carry

    lax.fori_loop(0, KV, one_group, 0, unroll=True)
    for c in range(QK // 128):
        heads = []
        for head in (2 * c, 2 * c + 1):
            heads.append(stacked_head(d_q, head) if head < HEADS else d_k[head - HEADS])
        u = jnp.concatenate(heads, axis=1)
        d_qkv_ref[:, 128 * c : 128 * (c + 1)] = rope(u, cos_ref[...], sin_ref[...], -1.0).astype(BF)
    for c in range(3):
        heads = [d_v[j] for j in range(2 * c, min(2 * c + 2, KV))]
        wide = jnp.concatenate(heads, axis=1) if len(heads) > 1 else heads[0]
        d_qkv_ref[:, QK + 128 * c : QK + 128 * c + wide.shape[1]] = wide.astype(BF)
    d_a = mult_nt(d_qkv_ref[:, :QK], w[:, :QK]) + mult_nt(d_qkv_ref[:, QK:], w[:, QK + D :])
    d_norm, d_gain = norm_back(x_ref[...].astype(F32), gains_ref[0:1], d_a)
    grad_ref[...] = d_h_ref[...] + d_norm
    d_gain_ref[...] = d_gain


FLIPS = (3, 1, 2, 0)


def block_copies(full, outs, sems, me, chunk):
    return [
        pltpu.make_async_copy(full.at[chunk, shard_at(me, flip, ROWS, 16)], out.at[chunk, pl.ds(0, ROWS)], sems.at[chunk, k])
        for k, (flip, out) in enumerate(zip(FLIPS, outs))
    ]


def down_grad_kernel(me_ref, dy_ref, act_ref, *refs):
    outs, full, sems = refs[-6:-2], refs[-2], refs[-1]
    copies = []
    for k, (flip, out) in enumerate(zip(FLIPS, outs)):
        part = act_ref[:, shard_at(me_ref[0], flip, FF // 4, 128)]
        for c in range(4):
            full[k, c] = mult(dy_ref[ROWS * c : ROWS * (c + 1), :], part).astype(BF)
            copies.append(pltpu.make_async_copy(full.at[k, c], out.at[c, pl.ds(0, ROWS)], sems.at[k, c]))
            copies[-1].start()
    wait_all(copies)


def wide_grad_kernel(me_ref, b_ref, d_ref, *refs):
    outs, full, sems = refs[-6:-2], refs[-2], refs[-1]
    copies = []
    for c in range(4):
        full[c] = mult(b_ref[...], d_ref[:, UNIT * c : UNIT * (c + 1)]).astype(BF)
        copies += block_copies(full, outs, sems, me_ref[0], c)
        start_all(copies[-4:])
    wait_all(copies)


def attention_grad_kernel(me_ref, a_ref, att_ref, d_qkv_ref, d_low_ref, gain_ref, *refs):
    outs, full, sems, gain_sems = refs[-7:-3], refs[-3], refs[-2], refs[-1]
    a, att = a_ref[...], att_ref[...]
    copies = []
    for k, (flip, out) in enumerate(zip(FLIPS, outs)):
        place = lax.bitwise_xor(me_ref[0], jnp.int32(flip))
        copies.append(pltpu.make_async_copy(gain_ref.at[place], out.at[0, pl.ds(ROWS, 16)], gain_sems.at[k]))
    start_all(copies)
    for c in range(4):
        if c < 2:
            block = mult(a, d_qkv_ref[:, UNIT * c : UNIT * (c + 1)])
        elif c == 2:
            block = jnp.concatenate([mult(a, d_qkv_ref[:, 2 * UNIT :]), mult(att, d_low_ref[:, : UNIT // 2])], axis=1)
        else:
            block = mult(att, d_low_ref[:, UNIT // 2 :])
        full[c] = block.astype(BF)
        copies += block_copies(full, outs, sems, me_ref[0], c)
        start_all(copies[-4:])
    wait_all(copies)


def place_all(first_place, second_place, pieces, full, done):
    size = full.shape[0] // 4
    for k, by in enumerate((0, 3, 1, 2)):
        place = lax.rem(first_place + by, 4)
        columns = pl.ds(pl.multiple_of(place * UNIT, 128), UNIT)
        for j, other in enumerate((0, 3, 1, 2)):
            rows = pl.ds(pl.multiple_of(lax.rem(second_place + other, 4) * size, 16), size)
            if k < 3:
                part = pieces[k][size * j : size * (j + 1), :]
            else:
                at = size * (j % 2)
                part = pieces[3 + j // 2][at : at + size, :]
            full[rows, columns] = part.astype(F32)
        done(k, place, columns)


def place_left_kernel(place_ref, *refs):
    pieces, (query_ref, key_ref, value_ref, proj_ref, gain_ref, up_ref, full, sems) = refs[:5], refs[5:]
    copies = []

    def send(k, place, columns):
        copies.append(pltpu.make_async_copy(full.at[pl.ds(0, ROWS), columns], up_ref.at[:, columns], sems.at[k]))
        copies[-1].start()

    place_all(place_ref[0], place_ref[1], pieces, full, send)
    rows = slice(ROWS + 16, 2 * ROWS + 16)
    query_ref[...] = full[rows, :D]
    key_ref[...] = full[rows, D:QK].T
    value_ref[...] = full[rows, QK:QKV].T
    proj_ref[...] = full[rows, QKV:]
    gain_ref[...] = full[2 * ROWS + 16 : 2 * ROWS + 24, :256]
    wait_all(copies)


def place_right_kernel(place_ref, *refs):
    pieces, (gate_ref, down_ref, full, sems) = refs[:5], refs[5:]
    copies = []

    def send(k, place, columns):
        rows = pl.ds(pl.multiple_of(place * ROWS, 16), ROWS)
        copies.append(pltpu.make_async_copy(full.at[pl.ds(0, ROWS), columns], gate_ref.at[:, columns], sems.at[0, k]))
        copies.append(pltpu.make_async_copy(full.at[pl.ds(ROWS + 16, ROWS), columns], down_ref.at[rows], sems.at[1, k]))
        start_all(copies[-2:])

    place_all(place_ref[1], place_ref[0], pieces, full, send)
    wait_all(copies)


def run(kernel, name, ins, specs, outs, scratch, flops, out_specs=None):
    moved = sum(a.size * a.dtype.itemsize for a in ins) + sum(o.size * o.dtype.itemsize for o in outs)
    return pl.pallas_call(
        kernel,
        name=name,
        out_shape=outs,
        in_specs=specs,
        out_specs=out_specs or [VMEM] * len(outs),
        scratch_shapes=scratch,
        cost_estimate=pl.CostEstimate(flops=flops, bytes_accessed=moved, transcendentals=0),
        compiler_params=pltpu.CompilerParams(vmem_limit_bytes=LIMIT),
    )(*ins)


def swap_cores(value):
    return lax.ppermute(value, "core", [(0, 1), (1, 0)])


def shift_y(value, by):
    place = [(y % 2) * 2 + y // 2 for y in range(4)]
    return lax.ppermute(value, ("y_lo", "y_hi"), [(place[y], place[(y + by) % 4]) for y in range(4)])


def in_order(parts):
    core = lax.axis_index("core") == 1
    low = lax.axis_index("y_lo") == 1
    near = [jnp.where(core, parts[k ^ 1], parts[k]) for k in range(4)]
    return jnp.stack([jnp.where(low, near[k ^ 2], near[k]) for k in range(4)])


def after(value, *others):
    return lax.optimization_barrier((value, *others))[0]


def add_low(*terms):
    total = terms[0].astype(F32)
    for term in terms[1:]:
        total = total + term.astype(F32)
    return total.astype(BF)


def shift_ring(value, axis, by):
    return lax.ppermute(value, axis, [(i, (i + by) % 4) for i in range(4)])


def halves(value):
    half = value.shape[0] // 2
    return value[:half], value[half:]


def ring_scatter(*parts):
    sent = []
    for value, axis in parts:
        place = lax.axis_index(axis)
        own, before, behind, across = [
            lax.dynamic_index_in_dim(value, lax.rem(place + by, 4), 0, keepdims=False) for by in (0, 3, 1, 2)
        ]
        top, bottom = halves(across)
        sent.append((axis, own, before, behind, shift_ring(top, axis, 1), shift_ring(bottom, axis, -1)))
    moved = []
    for axis, own, before, behind, top, bottom in sent:
        behind = jnp.concatenate([add_low(halves(behind)[0], top), halves(behind)[1]])
        before = jnp.concatenate([halves(before)[0], add_low(halves(before)[1], bottom)])
        moved.append((own, shift_ring(behind, axis, 1), shift_ring(before, axis, -1)))
    return [add_low(*terms) for terms in moved]


def ring_gather(*parts):
    first = [(value, axis, shift_ring(value, axis, 1), shift_ring(value, axis, -1)) for value, axis in parts]
    return [
        [value, before, behind, shift_ring(halves(before)[0], axis, 1), shift_ring(halves(behind)[1], axis, -1)]
        for value, axis, before, behind in first
    ]


def body(tokens, lengths, norm_attn, w_query, w_key, w_value, w_out, norm_mlp, w_gate, w_up, w_down, cotangent):
    low, core = lax.axis_index("y_lo"), lax.axis_index("core")
    me = (low * 2 + core).astype(jnp.int32)[None]
    first = [jnp.concatenate([w_query, w_key], axis=1), jnp.concatenate([w_out, w_value], axis=1)]
    far = [shift_y(first[0], 1), shift_y(first[1], -1)]
    near = [swap_cores(m) for m in first]
    own_gains = jnp.stack([norm_attn, norm_mlp])
    far_gains = shift_y(own_gains, 1)
    pair = jnp.stack([own_gains, far_gains])
    other = swap_cores(pair)
    gains = in_order([pair[0], other[0], pair[1], other[1]]).transpose(1, 0, 2).reshape(2, D).astype(F32)
    first = [piece for k in range(2) for piece in (first[k], near[k], far[k], swap_cores(far[k]))]
    near_wide = swap_cores(w_gate), swap_cores(w_up)
    near_down = swap_cores(w_down.T)
    held_gate, held_up = lax.optimization_barrier((w_gate, w_up, *far, other, near_down, *near_wide))[:2]
    far_gate, far_up = shift_y(held_gate, 1), shift_y(held_up, -1)

    slots = jnp.arange(T, dtype=jnp.int32)
    ends = jnp.cumsum(lengths[0])
    start = jnp.max(jnp.where(slots[:, None] >= ends[None, :], ends[None, :], 0), axis=1)
    freq = BASE ** (-jnp.arange(HEAD_DIM // 2, dtype=F32) * 2.0 / HEAD_DIM)
    angle = (slots - start).astype(F32)[:, None] * freq[None, :]
    cosine = jnp.tile(jnp.cos(angle), (1, 4))
    sine = jnp.sin(angle)
    sine = jnp.tile(jnp.concatenate([-sine, sine], axis=1), (1, 2))
    start = start[:, None]

    dma = pltpu.SemaphoreType.DMA
    q, k, v, p0, p1, p2, x, h, b_low, *turned = run(
        attention_kernel,
        "attention",
        (me, tokens[0].T, gains, cosine, sine, start, *first),
        [SMEM] + [VMEM] * 5 + [ANY] * 8,
        [
            shape(KV, GROUP * T, HEAD_DIM),
            shape(KV, T, HEAD_DIM),
            shape(KV, T, HEAD_DIM),
            *(shape(KV, STACK, BLOCK * (i + 1)) for i in range(BLOCKS)),
            shape(T, D),
            shape(T, D, dtype=F32),
            shape(T, D),
            *[shape(D, T)] * 3,
        ],
        [pltpu.VMEM((D, PACK), BF), pltpu.VMEM((KV, GROUP * T, HEAD_DIM), F32), pltpu.VMEM((T, T), F32), pltpu.VMEM((T, D), BF), dma((2, 4))],
        2 * T * D * 2560 + 4 * HEADS * T * T * 128,
    )
    held_down = after(w_down.T, b_low)
    far_down = (shift_y(held_down[: D // 2], 1), shift_y(held_down[D // 2 :], -1))
    held = [swap_cores(after(part, b_low)) for part in (far_gate, far_up)]
    wide = [w_gate, near_wide[0], far_gate, held[0], w_up, near_wide[1], far_up, held[1]]
    act, silu, slope = run(
        gate_kernel,
        "gate_up",
        (me, b_low, *wide),
        [SMEM, VMEM] + [ANY] * 8,
        [shape(T, FF)] * 3,
        [pltpu.VMEM((D, 2 * FF), BF), dma((2 * FF // CHUNK, 4))],
        4 * T * D * FF,
    )
    down = [w_down.T, near_down, *far_down, *(swap_cores(after(part, act)) for part in far_down)]
    down_blocks = run(
        down_grad_kernel,
        "down_grad",
        (me, cotangent[0].T, act, *far_down),
        [SMEM, VMEM, VMEM, ANY, ANY],
        [shape(4, ROWS + 16, UNIT)] * 4,
        [pltpu.VMEM((4, 4, ROWS, UNIT), BF), dma((4, 4))],
        2 * T * D * FF,
        [ANY] * 4,
    )
    down_got = [swap_cores(down_blocks[k]) for k in range(2)]
    down_theirs = [add_low(down_blocks[2][part], down_got[0][part]) for part in (slice(0, 2), slice(2, 4))]
    down_y = [shift_y(down_theirs[0], 1), shift_y(down_theirs[1], -1)]
    result, d_gate, d_up, d_h, d_low, d_gain_mlp = run(
        mlp_kernel,
        "mlp_back",
        (me, act, silu, slope, h, cotangent[0].T, gains, *down, *wide, *down_theirs),
        [SMEM] + [VMEM] * 6 + [ANY] * 16,
        [shape(T, D), shape(T, FF), shape(T, FF), shape(T, D, dtype=F32), shape(T, D), shape(1, D, dtype=F32)],
        [pltpu.VMEM((D, FF), BF), pltpu.VMEM((D, 2 * FF), BF), pltpu.VMEM((T, D), F32), dma((3, 6))],
        8 * T * D * FF,
    )
    wide_blocks, wide_got, held = [], [], down_y
    for name, d_part in (("gate_grad", d_gate), ("up_grad", d_up)):
        blocks = run(
            wide_grad_kernel,
            name,
            (me, turned[2], d_part, *held),
            [SMEM] + [VMEM] * 2 + [ANY] * len(held),
            [shape(4, ROWS + 16, UNIT)] * 4,
            [pltpu.VMEM((4, D, UNIT), BF), dma((4, 4))],
            2 * T * D * FF,
            [ANY] * 4,
        )
        wide_blocks.append(blocks)
        wide_got.append([swap_cores(blocks[k]) for k in range(2)])
        held = blocks[:1]
    wide_theirs = [
        [add_low(wide_blocks[k][2][part], wide_got[k][0][part]) for part in (slice(0, 2), slice(2, 4))] for k in range(2)
    ]
    wide_y = [[shift_y(parts[0], 1), shift_y(parts[1], -1)] for parts in wide_theirs]
    d_qkv, grad_input, d_gain_attn = run(
        attention_back_kernel,
        "attention_back",
        (me, x, gains, cosine, sine, d_low, d_h, q, k, v, p0, p1, p2, *first, *wide_theirs[0]),
        [SMEM] + [VMEM] * 12 + [ANY] * 10,
        [shape(T, QKV), shape(T, D, dtype=F32), shape(1, D, dtype=F32)],
        [
            pltpu.VMEM((D, PACK), BF),
            pltpu.VMEM((KV, GROUP * T, HEAD_DIM), BF),
            pltpu.VMEM((KV, GROUP * T, HEAD_DIM), F32),
            pltpu.VMEM((KV, T, HEAD_DIM), F32),
            pltpu.VMEM((KV, T, HEAD_DIM), F32),
            dma((2, 4)),
        ],
        2 * T * D * 2560 + 8 * HEADS * T * T * 128,
    )
    d_gains = jnp.concatenate([d_gain_attn, d_gain_mlp]).reshape(2, 4, ROWS).transpose(1, 0, 2)
    d_gains = jnp.pad(d_gains, ((0, 0), (0, 14), (0, UNIT - ROWS))).astype(BF)
    first_blocks = run(
        attention_grad_kernel,
        "attention_grad",
        (me, *turned[:2], d_qkv, d_low, d_gains, *wide_y[0], *wide_theirs[1]),
        [SMEM] + [VMEM] * 5 + [ANY] * 4,
        [shape(4, ROWS + 16, UNIT)] * 4,
        [pltpu.VMEM((4, D, UNIT), BF), dma((4, 4)), dma((4,))],
        2 * T * D * FF,
        [ANY] * 4,
    )
    first_got = [swap_cores(first_blocks[k]) for k in range(2)]
    first_theirs = [add_low(first_blocks[2][part], first_got[0][part]) for part in (slice(0, 2), slice(2, 4))]
    first_y = [shift_y(first_theirs[0], 1), shift_y(first_theirs[1], -1)]
    wide_y[1] = [after(part, first_theirs[0]) for part in wide_y[1]]
    sum_gate, sum_up = [add_low(wide_blocks[k][3], wide_got[k][1], jnp.concatenate(wide_y[k])) for k in range(2)]
    sum_down = add_low(down_blocks[3], down_got[1], after(jnp.concatenate(down_y), first_theirs[0]))
    sum_first = add_low(first_blocks[3], first_got[1], jnp.concatenate(first_y))
    result, grad_input, sum_first = lax.optimization_barrier((result.T, grad_input.T, sum_first))
    left = jnp.concatenate([sum_up, sum_first], axis=1)
    right = jnp.concatenate([sum_gate, sum_down], axis=1)
    left, right = ring_scatter((left, "z"), (right, "x"))
    left, right = ring_scatter((left.reshape(4, -1, UNIT), "x"), (right.reshape(4, -1, UNIT), "z"))
    both = jnp.stack([left, right])
    left, right = add_low(both, lax.ppermute(both, "y_hi", [(0, 1), (1, 0)]))
    left, right = ring_gather((left, "x"), (right, "z"))
    left, right = ring_gather((jnp.concatenate(left), "z"), (jnp.concatenate(right), "x"))

    places = jnp.stack([lax.axis_index("z"), lax.axis_index("x")]).astype(jnp.int32)
    specs = [SMEM] + [VMEM] * 5
    gate, down_grad = run(
        place_right_kernel,
        "place_gate_down",
        (places, *right),
        specs,
        [shape(ROWS, FF, dtype=F32), shape(D, UNIT, dtype=F32)],
        [pltpu.VMEM((2 * (ROWS + 16), FF), F32), dma((2, 4))],
        0,
        [ANY] * 2,
    )
    query, key, value, proj, gain, up = run(
        place_left_kernel,
        "place_up_attention",
        (places, *left),
        specs,
        [
            shape(ROWS, D, dtype=F32),
            shape(KV * HEAD_DIM, ROWS, dtype=F32),
            shape(KV * HEAD_DIM, ROWS, dtype=F32),
            shape(ROWS, D, dtype=F32),
            shape(8, 256, dtype=F32),
            shape(ROWS, FF, dtype=F32),
        ],
        [pltpu.VMEM((2 * (ROWS + 16), FF), F32), dma((4,))],
        0,
        [VMEM] * 5 + [ANY],
    )
    down_grad = down_grad.T
    return (result.T[None], grad_input.T[None], gain[0, :ROWS], query, key.T, value.T, proj, gain[1, :ROWS], gate, up, down_grad)


def solution(mesh):
    torus = Mesh(mesh.devices.reshape(2, 2, 4, 4, 2), EVERY)
    rows = P(EVERY, None, None)
    weight = P(SHARD, None)
    gain = P(SHARD)
    return jax.shard_map(
        body,
        mesh=torus,
        in_specs=(rows, P(EVERY, None), gain, weight, weight, weight, weight, gain, weight, weight, weight, rows),
        out_specs=(rows, rows, gain, weight, weight, weight, weight, gain, weight, weight, weight),
        check_vma=False,
    )
```

profile of v0, /device:TPU:0, one launch (start us, length us, event | category | flops | bytes accessed | tf_op | source)
XLA Modules:
  0.0 302.5 jit_solution(1705265018595734772)
XLA Ops:
  11.8 12.5 %collective-permute-done.3.refs_2_ = bf16[240,1280]{1,0:T(8,128)(2,1)} collective-permute-done((bf16[240,1280]{1,0:T(8,128)(2,1)S(1)}, bf16[240,1280]{1,0:T(8,128)(2,1)}, u32[]{:S(2)}, u32[]{:S(2)}) %collective-permute-start.3) | collective-permute-done | bytes 614432 | tf_op jit(solution)/shard_map/ppermute | solution.py:395
  24.6 1.8 collective-permute-done.6.refs_6_
  26.5 2.9 collective-permute-start.13
  33.3 16.1 %attention.1 = (bf16[5,1152,64]{2,1,0:T(8,128)(2,1)}, bf16[5,384,64]{2,1,0:T(8,128)(2,1)S(1)}, bf16[5,384,64]{2,1,0:T(8,128)(2,1)S(1)}, bf16[5,384,128]{2,1,0:T(...) custom-call(s32[1]{0:T(128)} %bitcast.me_ref, ...), custom_call_target="tpu_custom_call" | custom-call | flops 3019898880 | bytes 15393796 | tf_op jit(solution)/shard_map/attention/pallas_call | solution.py:377
  49.4 7.2 %collective-permute-done.13.refs_6_.refs_12_ = bf16[240,2560]{1,0:T(8,128)(2,1)} collective-permute-done((bf16[240,2560]{1,0:T(8,128)(2,1)}, bf16[240,2560]{1,0:T(8,128)(2,1)}, u32[]{:S(2)}, u32[]{:S(2)}) %collective-permute-start.13) | collective-permute-done | bytes 1228832 | tf_op jit(solution)/shard_map/ppermute | solution.py:395
  56.6 3.2 %collective-permute-done.11.refs_2_.refs_8_ = bf16[240,2560]{1,0:T(8,128)(2,1)} collective-permute-done((bf16[240,2560]{1,0:T(8,128)(2,1)S(1)}, bf16[240,2560]{1,0:T(8,128)(2,1)}, u32[]{:S(2)}, u32[]{:S(2)}) %collective-permute-start.11) | collective-permute-done | bytes 1228832 | tf_op jit(solution)/shard_map/ppermute | solution.py:395
  60.0 3.7 %collective-permute-start.16 = (bf16[480,640]{1,0:T(8,128)(2,1)S(1)}, bf16[480,640]{1,0:T(8,128)(2,1)S(1)}, u32[]{:S(2)}, u32[]{:S(2)}) collective-permute-start(bf16[480,640]{1,0:T(8,128)(2,1)S(1)} %get-tuple-element.180), channel_id=1, source_target_pairs={{0,65},{64,0},{1,64},{65,1},{2,67},{66,2},{3,66},{67,3},{4,69},{68... | collective-permute-start | bytes 1843208 | tf_op jit(solution)/shard_map/ppermute | solution.py:395
  65.8 9.7 %gate_up.1 = (bf16[384,2560]{1,0:T(8,128)(2,1)}, bf16[384,2560]{1,0:T(8,128)(2,1)}, bf16[384,2560]{1,0:T(8,128)(2,1)}) custom-call(s32[1]{0:T(128)} %bitcast.me_ref, bf16[384,960]{1,0:T(8,128)(2,1)S(1)} %copy-done.4, bf16[240,2560]{1,0:T(8,128)(2,1)S(1)} %copy-done, bf16[240,2560]{1,0:T(8,128)(2,1)} %collective-permute-done.8.refs_1_.refs_7_, ...), custom_call_target="tpu_custom_call" | custom-call | flops 3774873600 | bytes 16465924 | tf_op jit(solution)/shard_map/gate_up/pallas_call | solution.py:377
  75.5 1.9 collective-permute-done.15.refs_0_.refs_2_
  77.5 5.7 %down_grad.1 = (bf16[4,256,640]{2,1,0:T(8,128)(2,1)}, bf16[4,256,640]{2,1,0:T(8,128)(2,1)}, bf16[4,256,640]{2,1,0:T(8,128)(2,1)}, bf16[4,256,640]{2,1,0:T(8,128)(2,1)}) custom-call(s32[1]{0:T(128)} %bitcast.me_ref, bf16[960,384]{1,0:T(8,128)(2,1)S(1)} %bitcast.174, bf16[384,2560]{1,0:T(8,128)(2,1)} %get-tuple-element.77.act_ref, ...), custom_call_target="tpu_custom_call" | custom-call | flops 1887436800 | bytes 9175044 | tf_op jit(solution)/shard_map/down_grad/pallas_call | solution.py:377
  83.8 3.6 %collective-permute-done.19 = bf16[4,256,640]{2,1,0:T(8,128)(2,1)S(1)} collective-permute-done((bf16[4,256,640]{2,1,0:T(8,128)(2,1)}, bf16[4,256,640]{2,1,0:T(8,128)(2,1)S(1)}, u32[]{:S(2)}, u32[]{:S(2)}) %collective-permute-start.19) | collective-permute-done | bytes 1310752 | tf_op jit(solution)/shard_map/ppermute | solution.py:390
  89.1 3.7 %collective-permute-start.21 = (bf16[2,256,640]{2,1,0:T(8,128)(2,1)S(1)}, bf16[2,256,640]{2,1,0:T(8,128)(2,1)S(1)}, u32[]{:S(2)}, u32[]{:S(2)}) collective-permute-start(bf16[2,256,640]{2,1,0:T(8,128)(2,1)S(1)} %get-tuple-element.178.refs_15_), channel_id=1, source_target_pairs={{0,65},{64,0},{1,64},{65,1},{2,67},{66,2},{3,66},{67,3},{4,69},{68... | collective-permute-start | bytes 1966088 | tf_op jit(solution)/shard_map/ppermute | solution.py:395
  93.7 15.9 %mlp_back.1 = (bf16[384,960]{1,0:T(8,128)(2,1)}, bf16[384,2560]{1,0:T(8,128)(2,1)}, bf16[384,2560]{1,0:T(8,128)(2,1)}, f32[384,960]{1,0:T(8,128)}, bf16[384,960]{1,0:T(8,128)(2,1)}, /*index=5*/f32[1,960]{1,0:T(1,128)S(1)}) custom-call(s32[1]{0:T(128)} %bitcast.me_ref, bf16[384,2560]{1,0:T(8,128)(2,1)} %get-tuple-element.77.act_ref, ...), custom_call_target="tpu_custom_call" | custom-call | flops 7549747200 | bytes 31059204 | tf_op jit(solution)/shard_map/mlp_back/pallas_call | solution.py:377
  109.6 6.0 %gate_grad.1 = (bf16[4,256,640]{2,1,0:T(8,128)(2,1)}, bf16[4,256,640]{2,1,0:T(8,128)(2,1)}, bf16[4,256,640]{2,1,0:T(8,128)(2,1)}, bf16[4,256,640]{2,1,0:T(8,128)(2,1)}) custom-call(s32[1]{0:T(128)} %bitcast.me_ref, bf16[960,384]{1,0:T(8,128)(2,1)} %get-tuple-element.96.b_ref, bf16[384,2560]{1,0:T(8,128)(2,1)} %get-tuple-element.97.d_ref, ...), custom_call_target="tpu_custom_call" | custom-call | flops 1887436800 | bytes 9256964 | tf_op jit(solution)/shard_map/gate_grad/pallas_call | solution.py:377
  115.7 5.8 %up_grad.1 = (bf16[4,256,640]{2,1,0:T(8,128)(2,1)}, bf16[4,256,640]{2,1,0:T(8,128)(2,1)}, bf16[4,256,640]{2,1,0:T(8,128)(2,1)}, bf16[4,256,640]{2,1,0:T(8,128)(2,1)}) custom-call(s32[1]{0:T(128)} %bitcast.me_ref, bf16[960,384]{1,0:T(8,128)(2,1)S(1)} %copy-done.3, bf16[384,2560]{1,0:T(8,128)(2,1)} %get-tuple-element.106.d_ref, ...), custom_call_target="tpu_custom_call" | custom-call | flops 1887436800 | bytes 9256964 | tf_op jit(solution)/shard_map/up_grad/pallas_call | solution.py:377
  124.0 3.2 %collective-permute-start.24 = (bf16[2,256,640]{2,1,0:T(8,128)(2,1)}, bf16[2,256,640]{2,1,0:T(8,128)(2,1)S(1)}, u32[]{:S(2)}, u32[]{:S(2)}) collective-permute-start(bf16[2,256,640]{2,1,0:T(8,128)(2,1)} %get-tuple-element.176.refs_9_), channel_id=1, source_target_pairs={{0,65},{64,0},{1,64},{65,1},{2,67},{66,2},{3,66},{67,3},{4,69},{68... | collective-permute-start | bytes 1966088 | tf_op jit(solution)/shard_map/ppermute | solution.py:395
  127.3 16.7 %attention_back.1 = (bf16[384,1600]{1,0:T(8,128)(2,1)}, f32[384,960]{1,0:T(8,128)}, f32[1,960]{1,0:T(1,128)S(1)}) custom-call(s32[1]{0:T(128)} %bitcast.me_ref, bf16[384,960]{1,0:T(8,128)(2,1)} %get-tuple-element.87.x_ref, f32[2,960]{1,0:T(2,128)S(1)} %reshape.159.gains_ref, f32[384,128]{1,0:T(8,128)S(1)} %copy.44.cos_ref, f32[384,128]{1,0:T(8,128)S(1)} %copy.45.sin_ref, ...), custom_call_target="tpu_custom_call" | custom-call | flops 4152360960 | bytes 16461060 | tf_op jit(solution)/shard_map/attention_back/pallas_call | solution.py:377
  144.1 3.0 %add_convert_fusion.6 = (bf16[2,256,640]{2,1,0:T(8,128)(2,1)}, bf16[2,256,640]{2,1,0:T(8,128)(2,1)}) fusion(bf16[4,256,640]{2,1,0:T(8,128)(2,1)} %collective-permute-done.25, bf16[4,256,640]{2,1,0:T(8,128)(2,1)} %get-tuple-element.107), kind=kLoop, calls=%fused_computation.29 | loop fusion | flops 2621440 | bytes 3932160 | tf_op jit(solution)/shard_map/convert_element_type | solution.py:413
  147.2 6.5 %attention_grad.1 = (bf16[4,256,640]{2,1,0:T(8,128)(2,1)}, bf16[4,256,640]{2,1,0:T(8,128)(2,1)}, bf16[4,256,640]{2,1,0:T(8,128)(2,1)}, bf16[4,256,640]{2,1,0:T(8,128)(2,1)}) custom-call(s32[1]{0:T(128)} %bitcast.me_ref, bf16[960,384]{1,0:T(8,128)(2,1)} %get-tuple-element.101.a_ref, bf16[960,384]{1,0:T(8,128)(2,1)} %get-tuple-element.102.att_ref, ...), custom_call_target="tpu_custom_call" | custom-call | flops 1887436800 | bytes 11386884 | tf_op jit(solution)/shard_map/attention_grad/pallas_call | solution.py:377
  155.6 3.0 %collective-permute-start.32 = (bf16[2,256,640]{2,1,0:T(8,128)(2,1)S(1)}, bf16[2,256,640]{2,1,0:T(8,128)(2,1)S(1)}, u32[]{:S(2)}, u32[]{:S(2)}) collective-permute-start(bf16[2,256,640]{2,1,0:T(8,128)(2,1)S(1)} %copy-done.14), channel_id=1, source_target_pairs={{0,65},{64,0},{1,64},{65,1},{2,67},{66,2},{3,66},{67,3},{4,69},{68... | collective-permute-start | bytes 1966088 | tf_op jit(solution)/shard_map/ppermute | solution.py:395
  158.6 2.0 add_convert_fusion.1
  162.5 1.8 add_convert_fusion
  166.3 7.0 %collective-permute-done.31 = bf16[2,256,640]{2,1,0:T(8,128)(2,1)S(1)} collective-permute-done((bf16[2,256,640]{2,1,0:T(8,128)(2,1)S(1)}, bf16[2,256,640]{2,1,0:T(8,128)(2,1)S(1)}, u32[]{:S(2)}, u32[]{:S(2)}) %collective-permute-start.31) | collective-permute-done | bytes 655392 | tf_op jit(solution)/shard_map/ppermute | solution.py:395
  173.3 3.2 %collective-permute-start.29 = (bf16[2,256,640]{2,1,0:T(8,128)(2,1)S(1)}, bf16[2,256,640]{2,1,0:T(8,128)(2,1)S(1)}, u32[]{:S(2)}, u32[]{:S(2)}) collective-permute-start(bf16[2,256,640]{2,1,0:T(8,128)(2,1)S(1)} %get-tuple-element.173), channel_id=1, source_target_pairs={{0,65},{64,0},{1,64},{65,1},{2,67},{66,2},{3,66},{67,3},{4,69},{68... | collective-permute-start | bytes 1966088 | tf_op jit(solution)/shard_map/ppermute | solution.py:395
  176.6 2.8 collective-permute-start.45
  180.2 5.1 %collective-permute-done.45 = bf16[256,640]{1,0:T(8,128)(2,1)S(1)} collective-permute-done((bf16[256,640]{1,0:T(8,128)(2,1)S(1)}, bf16[256,640]{1,0:T(8,128)(2,1)S(1)}, u32[]{:S(2)}, u32[]{:S(2)}) %collective-permute-start.45) | collective-permute-done | bytes 327712 | tf_op jit(solution)/shard_map/ppermute | solution.py:417
  185.4 3.8 %collective-permute-start.46 = (bf16[512,640]{1,0:T(8,128)(2,1)S(1)}, bf16[512,640]{1,0:T(8,128)(2,1)S(1)}, u32[]{:S(2)}, u32[]{:S(2)}) collective-permute-start(bf16[512,640]{1,0:T(8,128)(2,1)S(1)} %pad_maximum_fusion.4), channel_id=1, source_target_pairs={{0,6},{2,0},{4,2},{6,4},{1,7},{3,1},{5,3},{7,5},{8,14},{10,8},{12,... | collective-permute-start | bytes 1966088 | tf_op jit(solution)/shard_map/ppermute | solution.py:417
  191.2 2.1 collective-permute-start.33
  193.3 2.2 collective-permute-start.35
  195.5 6.1 %collective-permute-done.33 = bf16[256,640]{1,0:T(8,128)(2,1)S(1)} collective-permute-done((bf16[256,640]{1,0:T(8,128)(2,1)S(1)}, bf16[256,640]{1,0:T(8,128)(2,1)S(1)}, u32[]{:S(2)}, u32[]{:S(2)}) %collective-permute-start.33) | collective-permute-done | bytes 327712 | tf_op jit(solution)/shard_map/ppermute | solution.py:417
  203.6 3.2 %collective-permute-start.36 = (bf16[512,640]{1,0:T(8,128)(2,1)}, bf16[512,640]{1,0:T(8,128)(2,1)}, u32[]{:S(2)}, u32[]{:S(2)}) collective-permute-start(bf16[512,640]{1,0:T(8,128)(2,1)} %pad_maximum_fusion.2), channel_id=1, source_target_pairs={{0,24},{8,0},{16,8},{24,16},{1,25},{9,1},{17,9},{25,17},{2,26},{10... | collective-permute-start | bytes 1966088 | tf_op jit(solution)/shard_map/ppermute | solution.py:417
  207.7 3.2 %collective-permute-start.49 = (bf16[64,640]{1,0:T(8,128)(2,1)S(1)}, bf16[64,640]{1,0:T(8,128)(2,1)}, u32[]{:S(2)}, u32[]{:S(2)}) collective-permute-start(bf16[64,640]{1,0:T(8,128)(2,1)S(1)} %get-tuple-element.194), channel_id=1, source_target_pairs={{0,24},{8,0},{16,8},{24,16},{1,25},{9,1},{17,9},{25,17},{2,26},{10... | collective-permute-start | bytes 245768 | tf_op jit(solution)/shard_map/ppermute | solution.py:417
  211.0 9.2 %collective-permute-done.47 = bf16[64,640]{1,0:T(8,128)(2,1)} collective-permute-done((bf16[64,640]{1,0:T(8,128)(2,1)}, bf16[64,640]{1,0:T(8,128)(2,1)}, u32[]{:S(2)}, u32[]{:S(2)}) %collective-permute-start.47) | collective-permute-done | bytes 81952 | tf_op jit(solution)/shard_map/ppermute | solution.py:417
  227.1 3.3 %collective-permute-start.50 = (bf16[128,640]{1,0:T(8,128)(2,1)S(1)}, bf16[128,640]{1,0:T(8,128)(2,1)S(1)}, u32[]{:S(2)}, u32[]{:S(2)}) collective-permute-start(bf16[128,640]{1,0:T(8,128)(2,1)S(1)} %pad_maximum_fusion.11), channel_id=1, source_target_pairs={{0,24},{8,0},{16,8},{24,16},{1,25},{9,1},{17,9},{25,17},{2,26},{10... | collective-permute-start | bytes 491528 | tf_op jit(solution)/shard_map/ppermute | solution.py:417
  232.3 1.8 collective-permute-start.40
  234.2 3.1 %collective-permute-done.38 = bf16[128,640]{1,0:T(8,128)(2,1)S(1)} collective-permute-done((bf16[128,640]{1,0:T(8,128)(2,1)S(1)}, bf16[128,640]{1,0:T(8,128)(2,1)S(1)}, u32[]{:S(2)}, u32[]{:S(2)}) %collective-permute-start.38) | collective-permute-done | bytes 163872 | tf_op jit(solution)/shard_map/ppermute | solution.py:417
  239.4 7.1 %collective-permute-done.51 = bf16[2,128,640]{2,1,0:T(8,128)(2,1)S(1)} collective-permute-done((bf16[2,128,640]{2,1,0:T(8,128)(2,1)S(1)}, bf16[2,128,640]{2,1,0:T(8,128)(2,1)S(1)}, u32[]{:S(2)}, u32[]{:S(2)}) %collective-permute-start.51) | collective-permute-done | bytes 327712 | tf_op jit(solution)/shard_map/ppermute | solution.py:592
  251.1 2.1 collective-permute-start.53
  254.6 2.1 collective-permute-start.63
  257.9 2.2 collective-permute-start.55
  260.2 3.2 %collective-permute-done.54 = bf16[64,640]{1,0:T(8,128)(2,1)S(1)} collective-permute-done((bf16[64,640]{1,0:T(8,128)(2,1)S(1)}, bf16[64,640]{1,0:T(8,128)(2,1)S(1)}, u32[]{:S(2)}, u32[]{:S(2)}) %collective-permute-start.54) | collective-permute-done | bytes 81952 | tf_op jit(solution)/shard_map/ppermute | solution.py:417
  264.5 2.2 collective-permute-start.57
  270.2 8.6 %collective-permute-done.56.refs_1_ = bf16[512,640]{1,0:T(8,128)(2,1)S(1)} collective-permute-done((bf16[512,640]{1,0:T(8,128)(2,1)S(1)}, bf16[512,640]{1,0:T(8,128)(2,1)S(1)}, u32[]{:S(2)}, u32[]{:S(2)}) %collective-permute-start.56) | collective-permute-done | bytes 655392 | tf_op jit(solution)/shard_map/ppermute | solution.py:417
  280.4 3.2 %collective-permute-start.59 = (bf16[256,640]{1,0:T(8,128)(2,1)}, bf16[256,640]{1,0:T(8,128)(2,1)}, u32[]{:S(2)}, u32[]{:S(2)}) collective-permute-start(bf16[256,640]{1,0:T(8,128)(2,1)} %slice.313), channel_id=1, source_target_pairs={{0,24},{8,0},{16,8},{24,16},{1,25},{9,1},{17,9},{25,17},{2,26},{10... | collective-permute-start | bytes 983048 | tf_op jit(solution)/shard_map/ppermute | solution.py:417
  288.6 3.0 copy.51
  291.6 2.3 copy.50
  293.8 4.2 %place_up_attention.1 = (f32[240,960]{1,0:T(8,128)}, f32[320,240]{1,0:T(8,128)}, f32[320,240]{1,0:T(8,128)}, f32[240,960]{1,0:T(8,128)}, f32[8,256]{1,0:T(8,128)S(1)}, /*index=5*/f32[240,2560]{1,0:T(8,128)}) custom-call(s32[2]{0:T(128)S(1)} %pad_add_fusion.place_ref, bf16[512,640]{1,0:T(8,128)(2,1)S(1)} %constant_dynamic-update-slice_fusion.refs_0_, ...), custom_call_target="tpu_custom_call" | custom-call | bytes 7544840 | tf_op jit(solution)/shard_map/place_up_attention/pallas_call | solution.py:377
  298.6 3.6 %place_gate_down.1 = (f32[240,2560]{1,0:T(8,128)}, f32[960,640]{1,0:T(8,128)}) custom-call(s32[2]{0:T(128)S(1)} %pad_add_fusion.place_ref, bf16[512,640]{1,0:T(8,128)(2,1)S(1)} %constant_dynamic-update-slice_fusion.5.refs_0_, bf16[512,640]{1,0:T(8,128)(2,1)S(1)} %collective-permute-done.64.refs_1_, bf16[512,640]{1,0:T(8,128)(2,1)} %copy-done.6, ...), custom_call_target="tpu_custom_call" | custom-call | bytes 7536648 | tf_op jit(solution)/shard_map/place_gate_down/pallas_call | solution.py:377
  (244 shorter events, 64.8 us)
Async XLA Ops:
  3.8 22.7 %collective-permute-start.9 = (bf16[960,640]{1,0:T(8,128)(2,1)}, bf16[960,640]{1,0:T(8,128)(2,1)}, u32[]{:S(2)}, u32[]{:S(2)}) collective-permute-start(bf16[960,640]{1,0:T(8,128)(2,1)} %bitcast.182), channel_id=1, source_target_pairs={{0,32},{32,0},{1,33},{33,1},{2,34},{34,2},{3,35},{35,3},{4,36},{36... | collective-permute-start | bytes 3686408 | tf_op jit(solution)/shard_map/ppermute | solution.py:390
  3.8 22.7 %collective-permute-start.10 = (bf16[240,2560]{1,0:T(8,128)(2,1)}, bf16[240,2560]{1,0:T(8,128)(2,1)}, u32[]{:S(2)}, u32[]{:S(2)}) collective-permute-start(bf16[240,2560]{1,0:T(8,128)(2,1)} %refs_10_.1), channel_id=1, source_target_pairs={{0,32},{32,0},{1,33},{33,1},{2,34},{34,2},{3,35},{35,3},{4,36},{36... | collective-permute-start | bytes 3686408 | tf_op jit(solution)/shard_map/ppermute | solution.py:390
  4.3 22.2 %collective-permute-start.8 = (bf16[240,2560]{1,0:T(8,128)(2,1)}, bf16[240,2560]{1,0:T(8,128)(2,1)}, u32[]{:S(2)}, u32[]{:S(2)}) collective-permute-start(bf16[240,2560]{1,0:T(8,128)(2,1)} %refs_6_.1), channel_id=1, source_target_pairs={{0,32},{32,0},{1,33},{33,1},{2,34},{34,2},{3,35},{35,3},{4,36},{36... | collective-permute-start | bytes 3686408 | tf_op jit(solution)/shard_map/ppermute | solution.py:390
  6.7 17.7 %collective-permute-start.3 = (bf16[240,1280]{1,0:T(8,128)(2,1)S(1)}, bf16[240,1280]{1,0:T(8,128)(2,1)}, u32[]{:S(2)}, u32[]{:S(2)}) collective-permute-start(bf16[240,1280]{1,0:T(8,128)(2,1)S(1)} %pad_maximum_fusion.5.refs_0_), channel_id=1, source_target_pairs={{0,64},{64,1},{1,65},{65,0},{2,66},{66,3},{3,67},{67,2},{4,68},{68... | collective-permute-start | bytes 1843208 | tf_op jit(solution)/shard_map/ppermute | solution.py:395
  10.2 16.2 %collective-permute-start.6 = (bf16[240,1280]{1,0:T(8,128)(2,1)}, bf16[240,1280]{1,0:T(8,128)(2,1)}, u32[]{:S(2)}, u32[]{:S(2)}) collective-permute-start(bf16[240,1280]{1,0:T(8,128)(2,1)} %pad_maximum_fusion.6.refs_4_), channel_id=1, source_target_pairs={{0,65},{64,0},{1,64},{65,1},{2,67},{66,2},{3,66},{67,3},{4,69},{68... | collective-permute-start | bytes 1843208 | tf_op jit(solution)/shard_map/ppermute | solution.py:395
  26.5 30.1 %collective-permute-start.13 = (bf16[240,2560]{1,0:T(8,128)(2,1)}, bf16[240,2560]{1,0:T(8,128)(2,1)}, u32[]{:S(2)}, u32[]{:S(2)}) collective-permute-start(bf16[240,2560]{1,0:T(8,128)(2,1)} %refs_10_.1), channel_id=1, source_target_pairs={{0,65},{64,0},{1,64},{65,1},{2,67},{66,2},{3,66},{67,3},{4,69},{68... | collective-permute-start | bytes 3686408 | tf_op jit(solution)/shard_map/ppermute | solution.py:395
  29.3 30.5 %collective-permute-start.11 = (bf16[240,2560]{1,0:T(8,128)(2,1)S(1)}, bf16[240,2560]{1,0:T(8,128)(2,1)}, u32[]{:S(2)}, u32[]{:S(2)}) collective-permute-start(bf16[240,2560]{1,0:T(8,128)(2,1)S(1)} %copy-done), channel_id=1, source_target_pairs={{0,64},{64,1},{1,65},{65,0},{2,66},{66,3},{3,67},{67,2},{4,68},{68... | collective-permute-start | bytes 3686408 | tf_op jit(solution)/shard_map/ppermute | solution.py:395
  56.6 7.1 %collective-permute-start.14 = (bf16[240,2560]{1,0:T(8,128)(2,1)}, bf16[240,2560]{1,0:T(8,128)(2,1)S(1)}, u32[]{:S(2)}, u32[]{:S(2)}) collective-permute-start(bf16[240,2560]{1,0:T(8,128)(2,1)} %collective-permute-done.13.refs_6_.refs_12_), channel_id=1, source_target_pairs={{0,32},{32,0},{1,33},{33,1},{2,34},{34,2},{3,35},{35,3},{4,36},{36... | collective-permute-start | bytes 3686408 | tf_op jit(solution)/shard_map/ppermute | solution.py:390
  59.9 17.5 %collective-permute-start.15 = (bf16[480,640]{1,0:T(8,128)(2,1)S(1)}, bf16[480,640]{1,0:T(8,128)(2,1)S(1)}, u32[]{:S(2)}, u32[]{:S(2)}) collective-permute-start(bf16[480,640]{1,0:T(8,128)(2,1)S(1)} %get-tuple-element.181), channel_id=1, source_target_pairs={{0,64},{64,1},{1,65},{65,0},{2,66},{66,3},{3,67},{67,2},{4,68},{68... | collective-permute-start | bytes 1843208 | tf_op jit(solution)/shard_map/ppermute | solution.py:395
  60.0 17.5 %collective-permute-start.16 = (bf16[480,640]{1,0:T(8,128)(2,1)S(1)}, bf16[480,640]{1,0:T(8,128)(2,1)S(1)}, u32[]{:S(2)}, u32[]{:S(2)}) collective-permute-start(bf16[480,640]{1,0:T(8,128)(2,1)S(1)} %get-tuple-element.180), channel_id=1, source_target_pairs={{0,65},{64,0},{1,64},{65,1},{2,67},{66,2},{3,66},{67,3},{4,69},{68... | collective-permute-start | bytes 1843208 | tf_op jit(solution)/shard_map/ppermute | solution.py:395
  83.2 9.6 %collective-permute-start.18 = (bf16[480,640]{1,0:T(8,128)(2,1)S(1)}, bf16[480,640]{1,0:T(8,128)(2,1)S(1)}, u32[]{:S(2)}, u32[]{:S(2)}) collective-permute-start(bf16[480,640]{1,0:T(8,128)(2,1)S(1)} %collective-permute-done.16.refs_1_.refs_3_), channel_id=1, source_target_pairs={{0,32},{32,0},{1,33},{33,1},{2,34},{34,2},{3,35},{35,3},{4,36},{36... | collective-permute-start | bytes 1843208 | tf_op jit(solution)/shard_map/ppermute | solution.py:390
  83.7 9.1 %collective-permute-start.17 = (bf16[480,640]{1,0:T(8,128)(2,1)S(1)}, bf16[480,640]{1,0:T(8,128)(2,1)S(1)}, u32[]{:S(2)}, u32[]{:S(2)}) collective-permute-start(bf16[480,640]{1,0:T(8,128)(2,1)S(1)} %collective-permute-done.15.refs_0_.refs_2_), channel_id=1, source_target_pairs={{0,32},{32,0},{1,33},{33,1},{2,34},{34,2},{3,35},{35,3},{4,36},{36... | collective-permute-start | bytes 1843208 | tf_op jit(solution)/shard_map/ppermute | solution.py:390
  89.1 20.5 %collective-permute-start.20 = (bf16[2,256,640]{2,1,0:T(8,128)(2,1)S(1)}, bf16[2,256,640]{2,1,0:T(8,128)(2,1)S(1)}, u32[]{:S(2)}, u32[]{:S(2)}) collective-permute-start(bf16[2,256,640]{2,1,0:T(8,128)(2,1)S(1)} %get-tuple-element.179.refs_14_), channel_id=1, source_target_pairs={{0,64},{64,1},{1,65},{65,0},{2,66},{66,3},{3,67},{67,2},{4,68},{68... | collective-permute-start | bytes 1966088 | tf_op jit(solution)/shard_map/ppermute | solution.py:395
  89.1 20.4 %collective-permute-start.21 = (bf16[2,256,640]{2,1,0:T(8,128)(2,1)S(1)}, bf16[2,256,640]{2,1,0:T(8,128)(2,1)S(1)}, u32[]{:S(2)}, u32[]{:S(2)}) collective-permute-start(bf16[2,256,640]{2,1,0:T(8,128)(2,1)S(1)} %get-tuple-element.178.refs_15_), channel_id=1, source_target_pairs={{0,65},{64,0},{1,64},{65,1},{2,67},{66,2},{3,66},{67,3},{4,69},{68... | collective-permute-start | bytes 1966088 | tf_op jit(solution)/shard_map/ppermute | solution.py:395
  121.5 22.6 %collective-permute-start.25 = (bf16[4,256,640]{2,1,0:T(8,128)(2,1)}, bf16[4,256,640]{2,1,0:T(8,128)(2,1)}, u32[]{:S(2)}, u32[]{:S(2)}) collective-permute-start(bf16[4,256,640]{2,1,0:T(8,128)(2,1)} %get-tuple-element.108), channel_id=1, source_target_pairs={{0,32},{32,0},{1,33},{33,1},{2,34},{34,2},{3,35},{35,3},{4,36},{36... | collective-permute-start | bytes 3932168 | tf_op jit(solution)/shard_map/ppermute | solution.py:390
  122.5 32.9 %collective-permute-start.41 = (bf16[4,256,640]{2,1,0:T(8,128)(2,1)}, bf16[4,256,640]{2,1,0:T(8,128)(2,1)}, u32[]{:S(2)}, u32[]{:S(2)}) collective-permute-start(bf16[4,256,640]{2,1,0:T(8,128)(2,1)} %get-tuple-element.121), channel_id=1, source_target_pairs={{0,32},{32,0},{1,33},{33,1},{2,34},{34,2},{3,35},{35,3},{4,36},{36... | collective-permute-start | bytes 3932168 | tf_op jit(solution)/shard_map/ppermute | solution.py:390
  124.0 23.1 %collective-permute-start.23 = (bf16[2,256,640]{2,1,0:T(8,128)(2,1)}, bf16[2,256,640]{2,1,0:T(8,128)(2,1)S(1)}, u32[]{:S(2)}, u32[]{:S(2)}) collective-permute-start(bf16[2,256,640]{2,1,0:T(8,128)(2,1)} %get-tuple-element.177.refs_8_), channel_id=1, source_target_pairs={{0,64},{64,1},{1,65},{65,0},{2,66},{66,3},{3,67},{67,2},{4,68},{68... | collective-permute-start | bytes 1966088 | tf_op jit(solution)/shard_map/ppermute | solution.py:395
  124.0 23.1 %collective-permute-start.24 = (bf16[2,256,640]{2,1,0:T(8,128)(2,1)}, bf16[2,256,640]{2,1,0:T(8,128)(2,1)S(1)}, u32[]{:S(2)}, u32[]{:S(2)}) collective-permute-start(bf16[2,256,640]{2,1,0:T(8,128)(2,1)} %get-tuple-element.176.refs_9_), channel_id=1, source_target_pairs={{0,65},{64,0},{1,64},{65,1},{2,67},{66,2},{3,66},{67,3},{4,69},{68... | collective-permute-start | bytes 1966088 | tf_op jit(solution)/shard_map/ppermute | solution.py:395
  153.8 8.7 %collective-permute-start.42 = (bf16[4,256,640]{2,1,0:T(8,128)(2,1)}, bf16[4,256,640]{2,1,0:T(8,128)(2,1)}, u32[]{:S(2)}, u32[]{:S(2)}) collective-permute-start(bf16[4,256,640]{2,1,0:T(8,128)(2,1)} %get-tuple-element.123), channel_id=1, source_target_pairs={{0,32},{32,0},{1,33},{33,1},{2,34},{34,2},{3,35},{35,3},{4,36},{36... | collective-permute-start | bytes 3932168 | tf_op jit(solution)/shard_map/ppermute | solution.py:390
  154.3 22.3 %collective-permute-start.30 = (bf16[4,256,640]{2,1,0:T(8,128)(2,1)}, bf16[4,256,640]{2,1,0:T(8,128)(2,1)S(1)}, u32[]{:S(2)}, u32[]{:S(2)}) collective-permute-start(bf16[4,256,640]{2,1,0:T(8,128)(2,1)} %get-tuple-element.116), channel_id=1, source_target_pairs={{0,32},{32,0},{1,33},{33,1},{2,34},{34,2},{3,35},{35,3},{4,36},{36... | collective-permute-start | bytes 3932168 | tf_op jit(solution)/shard_map/ppermute | solution.py:390
  155.4 17.9 %collective-permute-start.31 = (bf16[2,256,640]{2,1,0:T(8,128)(2,1)S(1)}, bf16[2,256,640]{2,1,0:T(8,128)(2,1)S(1)}, u32[]{:S(2)}, u32[]{:S(2)}) collective-permute-start(bf16[2,256,640]{2,1,0:T(8,128)(2,1)S(1)} %copy-done.15), channel_id=1, source_target_pairs={{0,64},{64,1},{1,65},{65,0},{2,66},{66,3},{3,67},{67,2},{4,68},{68... | collective-permute-start | bytes 1966088 | tf_op jit(solution)/shard_map/ppermute | solution.py:395
  155.6 17.8 %collective-permute-start.32 = (bf16[2,256,640]{2,1,0:T(8,128)(2,1)S(1)}, bf16[2,256,640]{2,1,0:T(8,128)(2,1)S(1)}, u32[]{:S(2)}, u32[]{:S(2)}) collective-permute-start(bf16[2,256,640]{2,1,0:T(8,128)(2,1)S(1)} %copy-done.14), channel_id=1, source_target_pairs={{0,65},{64,0},{1,64},{65,1},{2,67},{66,2},{3,66},{67,3},{4,69},{68... | collective-permute-start | bytes 1966088 | tf_op jit(solution)/shard_map/ppermute | solution.py:395
  160.6 28.5 %collective-permute-start.26 = (bf16[4,256,640]{2,1,0:T(8,128)(2,1)S(1)}, bf16[4,256,640]{2,1,0:T(8,128)(2,1)S(1)}, u32[]{:S(2)}, u32[]{:S(2)}) collective-permute-start(bf16[4,256,640]{2,1,0:T(8,128)(2,1)S(1)} %copy-done.21), channel_id=1, source_target_pairs={{0,32},{32,0},{1,33},{33,1},{2,34},{34,2},{3,35},{35,3},{4,36},{36... | collective-permute-start | bytes 3932168 | tf_op jit(solution)/shard_map/ppermute | solution.py:390
  164.6 15.4 %collective-permute-start.43 = (bf16[256,640]{1,0:T(8,128)(2,1)S(1)}, bf16[256,640]{1,0:T(8,128)(2,1)S(1)}, u32[]{:S(2)}, u32[]{:S(2)}) collective-permute-start(bf16[256,640]{1,0:T(8,128)(2,1)S(1)} %get-tuple-element.196), channel_id=1, source_target_pairs={{0,2},{2,4},{4,6},{6,0},{1,3},{3,5},{5,7},{7,1},{8,10},{10,12},{12... | collective-permute-start | bytes 983048 | tf_op jit(solution)/shard_map/ppermute | solution.py:417
  173.3 17.1 %collective-permute-start.28 = (bf16[2,256,640]{2,1,0:T(8,128)(2,1)S(1)}, bf16[2,256,640]{2,1,0:T(8,128)(2,1)S(1)}, u32[]{:S(2)}, u32[]{:S(2)}) collective-permute-start(bf16[2,256,640]{2,1,0:T(8,128)(2,1)S(1)} %get-tuple-element.172), channel_id=1, source_target_pairs={{0,64},{64,1},{1,65},{65,0},{2,66},{66,3},{3,67},{67,2},{4,68},{68... | collective-permute-start | bytes 1966088 | tf_op jit(solution)/shard_map/ppermute | solution.py:395
  173.3 17.1 %collective-permute-start.29 = (bf16[2,256,640]{2,1,0:T(8,128)(2,1)S(1)}, bf16[2,256,640]{2,1,0:T(8,128)(2,1)S(1)}, u32[]{:S(2)}, u32[]{:S(2)}) collective-permute-start(bf16[2,256,640]{2,1,0:T(8,128)(2,1)S(1)} %get-tuple-element.173), channel_id=1, source_target_pairs={{0,65},{64,0},{1,64},{65,1},{2,67},{66,2},{3,66},{67,3},{4,69},{68... | collective-permute-start | bytes 1966088 | tf_op jit(solution)/shard_map/ppermute | solution.py:395
  176.6 8.7 %collective-permute-start.45 = (bf16[256,640]{1,0:T(8,128)(2,1)S(1)}, bf16[256,640]{1,0:T(8,128)(2,1)S(1)}, u32[]{:S(2)}, u32[]{:S(2)}) collective-permute-start(bf16[256,640]{1,0:T(8,128)(2,1)S(1)} %get-tuple-element.197), channel_id=1, source_target_pairs={{0,6},{2,0},{4,2},{6,4},{1,7},{3,1},{5,3},{7,5},{8,14},{10,8},{12,... | collective-permute-start | bytes 983048 | tf_op jit(solution)/shard_map/ppermute | solution.py:417
  180.1 26.7 %collective-permute-start.44 = (bf16[512,640]{1,0:T(8,128)(2,1)S(1)}, bf16[512,640]{1,0:T(8,128)(2,1)S(1)}, u32[]{:S(2)}, u32[]{:S(2)}) collective-permute-start(bf16[512,640]{1,0:T(8,128)(2,1)S(1)} %pad_maximum_fusion.3), channel_id=1, source_target_pairs={{0,2},{2,4},{4,6},{6,0},{1,3},{3,5},{5,7},{7,1},{8,10},{10,12},{12... | collective-permute-start | bytes 1966088 | tf_op jit(solution)/shard_map/ppermute | solution.py:417
  185.4 21.4 %collective-permute-start.46 = (bf16[512,640]{1,0:T(8,128)(2,1)S(1)}, bf16[512,640]{1,0:T(8,128)(2,1)S(1)}, u32[]{:S(2)}, u32[]{:S(2)}) collective-permute-start(bf16[512,640]{1,0:T(8,128)(2,1)S(1)} %pad_maximum_fusion.4), channel_id=1, source_target_pairs={{0,6},{2,0},{4,2},{6,4},{1,7},{3,1},{5,3},{7,5},{8,14},{10,8},{12,... | collective-permute-start | bytes 1966088 | tf_op jit(solution)/shard_map/ppermute | solution.py:417
  191.2 10.4 %collective-permute-start.33 = (bf16[256,640]{1,0:T(8,128)(2,1)S(1)}, bf16[256,640]{1,0:T(8,128)(2,1)S(1)}, u32[]{:S(2)}, u32[]{:S(2)}) collective-permute-start(bf16[256,640]{1,0:T(8,128)(2,1)S(1)} %get-tuple-element.188), channel_id=1, source_target_pairs={{0,8},{8,16},{16,24},{24,0},{1,9},{9,17},{17,25},{25,1},{2,10},{10... | collective-permute-start | bytes 983048 | tf_op jit(solution)/shard_map/ppermute | solution.py:417
  193.3 9.3 %collective-permute-start.35 = (bf16[256,640]{1,0:T(8,128)(2,1)S(1)}, bf16[256,640]{1,0:T(8,128)(2,1)S(1)}, u32[]{:S(2)}, u32[]{:S(2)}) collective-permute-start(bf16[256,640]{1,0:T(8,128)(2,1)S(1)} %get-tuple-element.189), channel_id=1, source_target_pairs={{0,24},{8,0},{16,8},{24,16},{1,25},{9,1},{17,9},{25,17},{2,26},{10... | collective-permute-start | bytes 983048 | tf_op jit(solution)/shard_map/ppermute | solution.py:417
  202.6 19.4 %collective-permute-start.34 = (bf16[512,640]{1,0:T(8,128)(2,1)}, bf16[512,640]{1,0:T(8,128)(2,1)}, u32[]{:S(2)}, u32[]{:S(2)}) collective-permute-start(bf16[512,640]{1,0:T(8,128)(2,1)} %pad_maximum_fusion.1), channel_id=1, source_target_pairs={{0,8},{8,16},{16,24},{24,0},{1,9},{9,17},{17,25},{25,1},{2,10},{10... | collective-permute-start | bytes 1966088 | tf_op jit(solution)/shard_map/ppermute | solution.py:417
  203.6 18.4 %collective-permute-start.36 = (bf16[512,640]{1,0:T(8,128)(2,1)}, bf16[512,640]{1,0:T(8,128)(2,1)}, u32[]{:S(2)}, u32[]{:S(2)}) collective-permute-start(bf16[512,640]{1,0:T(8,128)(2,1)} %pad_maximum_fusion.2), channel_id=1, source_target_pairs={{0,24},{8,0},{16,8},{24,16},{1,25},{9,1},{17,9},{25,17},{2,26},{10... | collective-permute-start | bytes 1966088 | tf_op jit(solution)/shard_map/ppermute | solution.py:417
  207.7 12.5 %collective-permute-start.47 = (bf16[64,640]{1,0:T(8,128)(2,1)}, bf16[64,640]{1,0:T(8,128)(2,1)}, u32[]{:S(2)}, u32[]{:S(2)}) collective-permute-start(bf16[64,640]{1,0:T(8,128)(2,1)} %get-tuple-element.192), channel_id=1, source_target_pairs={{0,8},{8,16},{16,24},{24,0},{1,9},{9,17},{17,25},{25,1},{2,10},{10... | collective-permute-start | bytes 245768 | tf_op jit(solution)/shard_map/ppermute | solution.py:417
  207.7 12.6 %collective-permute-start.49 = (bf16[64,640]{1,0:T(8,128)(2,1)S(1)}, bf16[64,640]{1,0:T(8,128)(2,1)}, u32[]{:S(2)}, u32[]{:S(2)}) collective-permute-start(bf16[64,640]{1,0:T(8,128)(2,1)S(1)} %get-tuple-element.194), channel_id=1, source_target_pairs={{0,24},{8,0},{16,8},{24,16},{1,25},{9,1},{17,9},{25,17},{2,26},{10... | collective-permute-start | bytes 245768 | tf_op jit(solution)/shard_map/ppermute | solution.py:417
  221.3 12.8 %collective-permute-start.48 = (bf16[128,640]{1,0:T(8,128)(2,1)S(1)}, bf16[128,640]{1,0:T(8,128)(2,1)S(1)}, u32[]{:S(2)}, u32[]{:S(2)}) collective-permute-start(bf16[128,640]{1,0:T(8,128)(2,1)S(1)} %pad_maximum_fusion.10), channel_id=1, source_target_pairs={{0,8},{8,16},{16,24},{24,0},{1,9},{9,17},{17,25},{25,1},{2,10},{10... | collective-permute-start | bytes 491528 | tf_op jit(solution)/shard_map/ppermute | solution.py:417
  227.1 7.0 %collective-permute-start.50 = (bf16[128,640]{1,0:T(8,128)(2,1)S(1)}, bf16[128,640]{1,0:T(8,128)(2,1)S(1)}, u32[]{:S(2)}, u32[]{:S(2)}) collective-permute-start(bf16[128,640]{1,0:T(8,128)(2,1)S(1)} %pad_maximum_fusion.11), channel_id=1, source_target_pairs={{0,24},{8,0},{16,8},{24,16},{1,25},{9,1},{17,9},{25,17},{2,26},{10... | collective-permute-start | bytes 491528 | tf_op jit(solution)/shard_map/ppermute | solution.py:417
  237.9 8.7 %collective-permute-start.51 = (bf16[2,128,640]{2,1,0:T(8,128)(2,1)S(1)}, bf16[2,128,640]{2,1,0:T(8,128)(2,1)S(1)}, u32[]{:S(2)}, u32[]{:S(2)}) collective-permute-start(bf16[2,128,640]{2,1,0:T(8,128)(2,1)S(1)} %pad_maximum_fusion.7), channel_id=1, source_target_pairs={{0,1},{1,0},{2,3},{3,2},{4,5},{5,4},{6,7},{7,6},{8,9},{9,8},{10,11... | collective-permute-start | bytes 983048 | tf_op jit(solution)/shard_map/ppermute | solution.py:592
  253.3 13.4 %collective-permute-start.62 = (bf16[64,640]{1,0:T(8,128)(2,1)S(1)}, bf16[64,640]{1,0:T(8,128)(2,1)S(1)}, u32[]{:S(2)}, u32[]{:S(2)}) collective-permute-start(bf16[64,640]{1,0:T(8,128)(2,1)S(1)} %slice.314), channel_id=1, source_target_pairs={{0,8},{8,16},{16,24},{24,0},{1,9},{9,17},{17,25},{25,1},{2,10},{10... | collective-permute-start | bytes 245768 | tf_op jit(solution)/shard_map/ppermute | solution.py:417
  254.6 12.1 %collective-permute-start.63 = (bf16[64,640]{1,0:T(8,128)(2,1)S(1)}, bf16[64,640]{1,0:T(8,128)(2,1)S(1)}, u32[]{:S(2)}, u32[]{:S(2)}) collective-permute-start(bf16[64,640]{1,0:T(8,128)(2,1)S(1)} %slice.315), channel_id=1, source_target_pairs={{0,24},{8,0},{16,8},{24,16},{1,25},{9,1},{17,9},{25,17},{2,26},{10... | collective-permute-start | bytes 245768 | tf_op jit(solution)/shard_map/ppermute | solution.py:417
  263.4 15.4 %collective-permute-start.56 = (bf16[512,640]{1,0:T(8,128)(2,1)S(1)}, bf16[512,640]{1,0:T(8,128)(2,1)S(1)}, u32[]{:S(2)}, u32[]{:S(2)}) collective-permute-start(bf16[512,640]{1,0:T(8,128)(2,1)S(1)} %constant_dynamic-update-slice_fusion.refs_0_), channel_id=1, source_target_pairs={{0,8},{8,16},{16,24},{24,0},{1,9},{9,17},{17,25},{25,1},{2,10},{10... | collective-permute-start | bytes 1966088 | tf_op jit(solution)/shard_map/ppermute | solution.py:417
  264.5 15.0 %collective-permute-start.57 = (bf16[512,640]{1,0:T(8,128)(2,1)S(1)}, bf16[512,640]{1,0:T(8,128)(2,1)S(1)}, u32[]{:S(2)}, u32[]{:S(2)}) collective-permute-start(bf16[512,640]{1,0:T(8,128)(2,1)S(1)} %constant_dynamic-update-slice_fusion.refs_0_), channel_id=1, source_target_pairs={{0,24},{8,0},{16,8},{24,16},{1,25},{9,1},{17,9},{25,17},{2,26},{10... | collective-permute-start | bytes 1966088 | tf_op jit(solution)/shard_map/ppermute | solution.py:417
  266.8 16.8 %collective-permute-start.64 = (bf16[512,640]{1,0:T(8,128)(2,1)S(1)}, bf16[512,640]{1,0:T(8,128)(2,1)S(1)}, u32[]{:S(2)}, u32[]{:S(2)}) collective-permute-start(bf16[512,640]{1,0:T(8,128)(2,1)S(1)} %constant_dynamic-update-slice_fusion.5.refs_0_), channel_id=1, source_target_pairs={{0,2},{2,4},{4,6},{6,0},{1,3},{3,5},{5,7},{7,1},{8,10},{10,12},{12... | collective-permute-start | bytes 1966088 | tf_op jit(solution)/shard_map/ppermute | solution.py:417
  268.5 17.5 %collective-permute-start.65 = (bf16[512,640]{1,0:T(8,128)(2,1)S(1)}, bf16[512,640]{1,0:T(8,128)(2,1)S(1)}, u32[]{:S(2)}, u32[]{:S(2)}) collective-permute-start(bf16[512,640]{1,0:T(8,128)(2,1)S(1)} %constant_dynamic-update-slice_fusion.5.refs_0_), channel_id=1, source_target_pairs={{0,6},{2,0},{4,2},{6,4},{1,7},{3,1},{5,3},{7,5},{8,14},{10,8},{12,... | collective-permute-start | bytes 1966088 | tf_op jit(solution)/shard_map/ppermute | solution.py:417
  279.5 14.3 %collective-permute-start.58 = (bf16[256,640]{1,0:T(8,128)(2,1)}, bf16[256,640]{1,0:T(8,128)(2,1)S(1)}, u32[]{:S(2)}, u32[]{:S(2)}) collective-permute-start(bf16[256,640]{1,0:T(8,128)(2,1)} %slice.312), channel_id=1, source_target_pairs={{0,8},{8,16},{16,24},{24,0},{1,9},{9,17},{17,25},{25,1},{2,10},{10... | collective-permute-start | bytes 983048 | tf_op jit(solution)/shard_map/ppermute | solution.py:417
  280.4 13.5 %collective-permute-start.59 = (bf16[256,640]{1,0:T(8,128)(2,1)}, bf16[256,640]{1,0:T(8,128)(2,1)}, u32[]{:S(2)}, u32[]{:S(2)}) collective-permute-start(bf16[256,640]{1,0:T(8,128)(2,1)} %slice.313), channel_id=1, source_target_pairs={{0,24},{8,0},{16,8},{24,16},{1,25},{9,1},{17,9},{25,17},{2,26},{10... | collective-permute-start | bytes 983048 | tf_op jit(solution)/shard_map/ppermute | solution.py:417
  284.4 14.3 %collective-permute-start.66 = (bf16[256,640]{1,0:T(8,128)(2,1)}, bf16[256,640]{1,0:T(8,128)(2,1)S(1)}, u32[]{:S(2)}, u32[]{:S(2)}) collective-permute-start(bf16[256,640]{1,0:T(8,128)(2,1)} %slice.316), channel_id=1, source_target_pairs={{0,2},{2,4},{4,6},{6,0},{1,3},{3,5},{5,7},{7,1},{8,10},{10,12},{12... | collective-permute-start | bytes 983048 | tf_op jit(solution)/shard_map/ppermute | solution.py:417
  286.9 11.8 %collective-permute-start.67 = (bf16[256,640]{1,0:T(8,128)(2,1)}, bf16[256,640]{1,0:T(8,128)(2,1)}, u32[]{:S(2)}, u32[]{:S(2)}) collective-permute-start(bf16[256,640]{1,0:T(8,128)(2,1)} %slice.317), channel_id=1, source_target_pairs={{0,6},{2,0},{4,2},{6,4},{1,7},{3,1},{5,3},{7,5},{8,14},{10,8},{12,... | collective-permute-start | bytes 983048 | tf_op jit(solution)/shard_map/ppermute | solution.py:417
  (47 other events, 331.3 us)
where the time goes:
time: 307 us; the launch traced here: 302 us
  Pallas kernels  90.2 us (29%)
  starting transfers between devices  87.3 us (28%)
  waiting for transfers between devices  83.5 us (27%)
  other arithmetic  21.4 us (7%)
  local copies, waits for them, and re-layouts  18.3 us (6%)
    pallas_call x10, Pallas kernels, run(): pl.pallas_call(kernel, name=name, out_shape=outs, in_specs=specs, out_spe...  90.2 us
    ppermute x32, starting transfers between devices, shift_ring(): return lax.ppermute(value, axis, [(i, (i + by) % 4) for i in range(4)])  56.6 us
    ppermute x32, waiting for transfers between devices, shift_ring(): return lax.ppermute(value, axis, [(i, (i + by) % 4) for i in range(4)])  36 us
    ppermute x15, waiting for transfers between devices, shift_y(): lax.ppermute(value, ('y_lo', 'y_hi'), [(place[y], place[(y + by) % 4]) fo...  35 us
    ppermute x15, starting transfers between devices, shift_y(): lax.ppermute(value, ('y_lo', 'y_hi'), [(place[y], place[(y + by) % 4]) fo...  24.9 us
    convert_element_type x17, other arithmetic, add_low(): return total.astype(BF)  15.8 us
    unnamed x65, local copies, waits for them, and re-layouts  11.5 us
    ppermute x1, waiting for transfers between devices, body(): left, right = add_low(both, lax.ppermute(both, 'y_hi', [(0, 1), (1, 0)]))  7.11 us
  transfers between devices with their start and end apart: 68, of which 20 were waited for; matrix products, arithmetic and copies ran while one was open for 11% of the time, Pallas kernels for 25%

commit v1 on v0

--- a/solution.py
+++ b/solution.py
@@ -324,51 +324,50 @@
     wait_all(copies)
 
 
-def place_all(first_place, second_place, pieces, full, done):
+def place_all(first_place, second_place, pieces, held, full, done):
     size = full.shape[0] // 4
     for k, by in enumerate((0, 3, 1, 2)):
+        wait_all(pieces[k : k + 1] if k < 3 else pieces[3:])
         place = lax.rem(first_place + by, 4)
         columns = pl.ds(pl.multiple_of(place * UNIT, 128), UNIT)
         for j, other in enumerate((0, 3, 1, 2)):
             rows = pl.ds(pl.multiple_of(lax.rem(second_place + other, 4) * size, 16), size)
-            if k < 3:
-                part = pieces[k][size * j : size * (j + 1), :]
-            else:
-                at = size * (j % 2)
-                part = pieces[3 + j // 2][at : at + size, :]
-            full[rows, columns] = part.astype(F32)
+            full[rows, columns] = held[k, size * j : size * (j + 1), :].astype(F32)
         done(k, place, columns)
 
 
-def place_left_kernel(place_ref, *refs):
-    pieces, (query_ref, key_ref, value_ref, proj_ref, gain_ref, up_ref, full, sems) = refs[:5], refs[5:]
+def piece_copies(pieces, held, sems):
+    half = held.shape[1] // 2
+    targets = [held.at[k] for k in range(3)] + [held.at[3, pl.ds(0, half)], held.at[3, pl.ds(half, half)]]
+    return [pltpu.make_async_copy(piece, target, sems.at[k]) for k, (piece, target) in enumerate(zip(pieces, targets))]
+
+
+def place_kernel(place_ref, *refs):
+    left, right, refs = refs[:5], refs[5:10], refs[10:]
+    (query_ref, key_ref, value_ref, proj_ref, gain_ref, up_ref, gate_ref, down_ref, held, full_left, full_right, sems, out_sems) = refs
+    right = piece_copies(right, held.at[1], sems.at[1])
+    left = piece_copies(left, held.at[0], sems.at[0])
+    start_all(right + left)
     copies = []
 
-    def send(k, place, columns):
-        copies.append(pltpu.make_async_copy(full.at[pl.ds(0, ROWS), columns], up_ref.at[:, columns], sems.at[k]))
+    def send_right(k, place, columns):
+        rows = pl.ds(pl.multiple_of(place * ROWS, 16), ROWS)
+        copies.append(pltpu.make_async_copy(full_right.at[pl.ds(0, ROWS), columns], gate_ref.at[:, columns], out_sems.at[0, k]))
+        copies.append(pltpu.make_async_copy(full_right.at[pl.ds(ROWS + 16, ROWS), columns], down_ref.at[rows], out_sems.at[1, k]))
+        start_all(copies[-2:])
+
+    def send_left(k, place, columns):
+        copies.append(pltpu.make_async_copy(full_left.at[pl.ds(0, ROWS), columns], up_ref.at[:, columns], out_sems.at[2, k]))
         copies[-1].start()
 
-    place_all(place_ref[0], place_ref[1], pieces, full, send)
+    place_all(place_ref[1], place_ref[0], right, held.at[1], full_right, send_right)
+    place_all(place_ref[0], place_ref[1], left, held.at[0], full_left, send_left)
     rows = slice(ROWS + 16, 2 * ROWS + 16)
-    query_ref[...] = full[rows, :D]
-    key_ref[...] = full[rows, D:QK].T
-    value_ref[...] = full[rows, QK:QKV].T
-    proj_ref[...] = full[rows, QKV:]
-    gain_ref[...] = full[2 * ROWS + 16 : 2 * ROWS + 24, :256]
-    wait_all(copies)
-
-
-def place_right_kernel(place_ref, *refs):
-    pieces, (gate_ref, down_ref, full, sems) = refs[:5], refs[5:]
-    copies = []
-
-    def send(k, place, columns):
-        rows = pl.ds(pl.multiple_of(place * ROWS, 16), ROWS)
-        copies.append(pltpu.make_async_copy(full.at[pl.ds(0, ROWS), columns], gate_ref.at[:, columns], sems.at[0, k]))
-        copies.append(pltpu.make_async_copy(full.at[pl.ds(ROWS + 16, ROWS), columns], down_ref.at[rows], sems.at[1, k]))
-        start_all(copies[-2:])
-
-    place_all(place_ref[1], place_ref[0], pieces, full, send)
+    query_ref[...] = full_left[rows, :D]
+    key_ref[...] = full_left[rows, D:QK].T
+    value_ref[...] = full_left[rows, QK:QKV].T
+    proj_ref[...] = full_left[rows, QKV:]
+    gain_ref[...] = full_left[2 * ROWS + 16 : 2 * ROWS + 24, :256]
     wait_all(copies)
 
 
@@ -594,22 +593,11 @@
     left, right = ring_gather((jnp.concatenate(left), "z"), (jnp.concatenate(right), "x"))
 
     places = jnp.stack([lax.axis_index("z"), lax.axis_index("x")]).astype(jnp.int32)
-    specs = [SMEM] + [VMEM] * 5
-    gate, down_grad = run(
-        place_right_kernel,
-        "place_gate_down",
-        (places, *right),
-        specs,
-        [shape(ROWS, FF, dtype=F32), shape(D, UNIT, dtype=F32)],
-        [pltpu.VMEM((2 * (ROWS + 16), FF), F32), dma((2, 4))],
-        0,
-        [ANY] * 2,
-    )
-    query, key, value, proj, gain, up = run(
-        place_left_kernel,
-        "place_up_attention",
-        (places, *left),
-        specs,
+    query, key, value, proj, gain, up, gate, down_grad = run(
+        place_kernel,
+        "place_gradients",
+        (places, *left, *right),
+        [SMEM] + [ANY] * 10,
         [
             shape(ROWS, D, dtype=F32),
             shape(KV * HEAD_DIM, ROWS, dtype=F32),
@@ -617,10 +605,18 @@
             shape(ROWS, D, dtype=F32),
             shape(8, 256, dtype=F32),
             shape(ROWS, FF, dtype=F32),
+            shape(ROWS, FF, dtype=F32),
+            shape(D, UNIT, dtype=F32),
         ],
-        [pltpu.VMEM((2 * (ROWS + 16), FF), F32), dma((4,))],
+        [
+            pltpu.VMEM((2, 4, 2 * (ROWS + 16), UNIT), BF),
+            pltpu.VMEM((2 * (ROWS + 16), FF), F32),
+            pltpu.VMEM((2 * (ROWS + 16), FF), F32),
+            dma((2, 5)),
+            dma((3, 4)),
+        ],
         0,
-        [VMEM] * 5 + [ANY],
+        [VMEM] * 5 + [ANY] * 3,
     )
     down_grad = down_grad.T
     return (result.T[None], grad_input.T[None], gain[0, :ROWS], query, key.T, value.T, proj, gain[1, :ROWS], gate, up, down_grad)

time: 307 us -> 305 us (level)
    pallas_call x10 -> x9, Pallas kernels: 90.2 us -> 88.7 us  [run(): pl.pallas_call(kernel, name=name, out_shape=outs, in_specs=specs, out_spe...]
    unnamed x65 -> x73, local copies, waits for them, and re-layouts: 11.5 us -> 10.9 us
  transfers between devices with their start and end apart: 68 -> 68, of which waited for: 20 -> 22; matrix products, arithmetic and copies ran while one was open for 11% -> 10% of each run, Pallas kernels for 25% -> 24%
where the time goes in v1:
time: 305 us; the launch traced here: 300 us
  Pallas kernels  88.7 us (29%)
  starting transfers between devices  87.2 us (29%)
  waiting for transfers between devices  83.3 us (27%)
  other arithmetic  21.4 us (7%)
  local copies, waits for them, and re-layouts  17.8 us (6%)
    pallas_call x9, Pallas kernels, run(): pl.pallas_call(kernel, name=name, out_shape=outs, in_specs=specs, out_spe...  88.7 us
    ppermute x32, starting transfers between devices, shift_ring(): return lax.ppermute(value, axis, [(i, (i + by) % 4) for i in range(4)])  56.5 us
    ppermute x32, waiting for transfers between devices, shift_ring(): return lax.ppermute(value, axis, [(i, (i + by) % 4) for i in range(4)])  35.8 us
    ppermute x15, waiting for transfers between devices, shift_y(): lax.ppermute(value, ('y_lo', 'y_hi'), [(place[y], place[(y + by) % 4]) fo...  35 us
    ppermute x15, starting transfers between devices, shift_y(): lax.ppermute(value, ('y_lo', 'y_hi'), [(place[y], place[(y + by) % 4]) fo...  24.9 us
    convert_element_type x17, other arithmetic, add_low(): return total.astype(BF)  15.8 us
    unnamed x73, local copies, waits for them, and re-layouts  10.9 us
    ppermute x1, waiting for transfers between devices, body(): left, right = add_low(both, lax.ppermute(both, 'y_hi', [(0, 1), (1, 0)]))  7.11 us
  transfers between devices with their start and end apart: 68, of which 22 were waited for; matrix products, arithmetic and copies ran while one was open for 10% of the time, Pallas kernels for 24%

profile of v1, /device:TPU:0, one launch (start us, length us, event | category | flops | bytes accessed | tf_op | source)
XLA Modules:
  0.0 300.2 jit_solution(14493924235671995488)
XLA Ops:
  11.8 12.5 %collective-permute-done.3.refs_2_ = bf16[240,1280]{1,0:T(8,128)(2,1)} collective-permute-done((bf16[240,1280]{1,0:T(8,128)(2,1)S(1)}, bf16[240,1280]{1,0:T(8,128)(2,1)}, u32[]{:S(2)}, u32[]{:S(2)}) %collective-permute-start.3) | collective-permute-done | bytes 614432 | tf_op jit(solution)/shard_map/ppermute | solution.py:394
  24.6 1.8 collective-permute-done.6.refs_6_
  26.5 2.9 collective-permute-start.13
  33.3 16.1 %attention.1 = (bf16[5,1152,64]{2,1,0:T(8,128)(2,1)}, bf16[5,384,64]{2,1,0:T(8,128)(2,1)S(1)}, bf16[5,384,64]{2,1,0:T(8,128)(2,1)S(1)}, bf16[5,384,128]{2,1,0:T(...) custom-call(s32[1]{0:T(128)} %bitcast.me_ref, ...), custom_call_target="tpu_custom_call" | custom-call | flops 3019898880 | bytes 15393796 | tf_op jit(solution)/shard_map/attention/pallas_call | solution.py:376
  49.4 7.2 %collective-permute-done.13.refs_6_.refs_12_ = bf16[240,2560]{1,0:T(8,128)(2,1)} collective-permute-done((bf16[240,2560]{1,0:T(8,128)(2,1)}, bf16[240,2560]{1,0:T(8,128)(2,1)}, u32[]{:S(2)}, u32[]{:S(2)}) %collective-permute-start.13) | collective-permute-done | bytes 1228832 | tf_op jit(solution)/shard_map/ppermute | solution.py:394
  56.6 3.2 %collective-permute-done.11.refs_2_.refs_8_ = bf16[240,2560]{1,0:T(8,128)(2,1)} collective-permute-done((bf16[240,2560]{1,0:T(8,128)(2,1)S(1)}, bf16[240,2560]{1,0:T(8,128)(2,1)}, u32[]{:S(2)}, u32[]{:S(2)}) %collective-permute-start.11) | collective-permute-done | bytes 1228832 | tf_op jit(solution)/shard_map/ppermute | solution.py:394
  60.0 3.7 %collective-permute-start.16 = (bf16[480,640]{1,0:T(8,128)(2,1)S(1)}, bf16[480,640]{1,0:T(8,128)(2,1)S(1)}, u32[]{:S(2)}, u32[]{:S(2)}) collective-permute-start(bf16[480,640]{1,0:T(8,128)(2,1)S(1)} %get-tuple-element.180), channel_id=1, source_target_pairs={{0,65},{64,0},{1,64},{65,1},{2,67},{66,2},{3,66},{67,3},{4,69},{68... | collective-permute-start | bytes 1843208 | tf_op jit(solution)/shard_map/ppermute | solution.py:394
  65.8 9.7 %gate_up.1 = (bf16[384,2560]{1,0:T(8,128)(2,1)}, bf16[384,2560]{1,0:T(8,128)(2,1)}, bf16[384,2560]{1,0:T(8,128)(2,1)}) custom-call(s32[1]{0:T(128)} %bitcast.me_ref, bf16[384,960]{1,0:T(8,128)(2,1)S(1)} %copy-done.4, bf16[240,2560]{1,0:T(8,128)(2,1)S(1)} %copy-done, bf16[240,2560]{1,0:T(8,128)(2,1)} %collective-permute-done.8.refs_1_.refs_7_, ...), custom_call_target="tpu_custom_call" | custom-call | flops 3774873600 | bytes 16465924 | tf_op jit(solution)/shard_map/gate_up/pallas_call | solution.py:376
  75.6 1.9 collective-permute-done.15.refs_0_.refs_2_
  77.5 5.7 %down_grad.1 = (bf16[4,256,640]{2,1,0:T(8,128)(2,1)}, bf16[4,256,640]{2,1,0:T(8,128)(2,1)}, bf16[4,256,640]{2,1,0:T(8,128)(2,1)}, bf16[4,256,640]{2,1,0:T(8,128)(2,1)}) custom-call(s32[1]{0:T(128)} %bitcast.me_ref, bf16[960,384]{1,0:T(8,128)(2,1)S(1)} %bitcast.174, bf16[384,2560]{1,0:T(8,128)(2,1)} %get-tuple-element.77.act_ref, ...), custom_call_target="tpu_custom_call" | custom-call | flops 1887436800 | bytes 9175044 | tf_op jit(solution)/shard_map/down_grad/pallas_call | solution.py:376
  83.8 3.6 %collective-permute-done.19 = bf16[4,256,640]{2,1,0:T(8,128)(2,1)S(1)} collective-permute-done((bf16[4,256,640]{2,1,0:T(8,128)(2,1)}, bf16[4,256,640]{2,1,0:T(8,128)(2,1)S(1)}, u32[]{:S(2)}, u32[]{:S(2)}) %collective-permute-start.19) | collective-permute-done | bytes 1310752 | tf_op jit(solution)/shard_map/ppermute | solution.py:389
  89.1 3.7 %collective-permute-start.21 = (bf16[2,256,640]{2,1,0:T(8,128)(2,1)S(1)}, bf16[2,256,640]{2,1,0:T(8,128)(2,1)S(1)}, u32[]{:S(2)}, u32[]{:S(2)}) collective-permute-start(bf16[2,256,640]{2,1,0:T(8,128)(2,1)S(1)} %get-tuple-element.178.refs_15_), channel_id=1, source_target_pairs={{0,65},{64,0},{1,64},{65,1},{2,67},{66,2},{3,66},{67,3},{4,69},{68... | collective-permute-start | bytes 1966088 | tf_op jit(solution)/shard_map/ppermute | solution.py:394
  93.7 15.9 %mlp_back.1 = (bf16[384,960]{1,0:T(8,128)(2,1)}, bf16[384,2560]{1,0:T(8,128)(2,1)}, bf16[384,2560]{1,0:T(8,128)(2,1)}, f32[384,960]{1,0:T(8,128)}, bf16[384,960]{1,0:T(8,128)(2,1)}, /*index=5*/f32[1,960]{1,0:T(1,128)S(1)}) custom-call(s32[1]{0:T(128)} %bitcast.me_ref, bf16[384,2560]{1,0:T(8,128)(2,1)} %get-tuple-element.77.act_ref, ...), custom_call_target="tpu_custom_call" | custom-call | flops 7549747200 | bytes 31059204 | tf_op jit(solution)/shard_map/mlp_back/pallas_call | solution.py:376
  109.6 6.0 %gate_grad.1 = (bf16[4,256,640]{2,1,0:T(8,128)(2,1)}, bf16[4,256,640]{2,1,0:T(8,128)(2,1)}, bf16[4,256,640]{2,1,0:T(8,128)(2,1)}, bf16[4,256,640]{2,1,0:T(8,128)(2,1)}) custom-call(s32[1]{0:T(128)} %bitcast.me_ref, bf16[960,384]{1,0:T(8,128)(2,1)} %get-tuple-element.96.b_ref, bf16[384,2560]{1,0:T(8,128)(2,1)} %get-tuple-element.97.d_ref, ...), custom_call_target="tpu_custom_call" | custom-call | flops 1887436800 | bytes 9256964 | tf_op jit(solution)/shard_map/gate_grad/pallas_call | solution.py:376
  115.7 5.8 %up_grad.1 = (bf16[4,256,640]{2,1,0:T(8,128)(2,1)}, bf16[4,256,640]{2,1,0:T(8,128)(2,1)}, bf16[4,256,640]{2,1,0:T(8,128)(2,1)}, bf16[4,256,640]{2,1,0:T(8,128)(2,1)}) custom-call(s32[1]{0:T(128)} %bitcast.me_ref, bf16[960,384]{1,0:T(8,128)(2,1)S(1)} %copy-done.3, bf16[384,2560]{1,0:T(8,128)(2,1)} %get-tuple-element.106.d_ref, ...), custom_call_target="tpu_custom_call" | custom-call | flops 1887436800 | bytes 9256964 | tf_op jit(solution)/shard_map/up_grad/pallas_call | solution.py:376
  124.0 3.2 %collective-permute-start.24 = (bf16[2,256,640]{2,1,0:T(8,128)(2,1)}, bf16[2,256,640]{2,1,0:T(8,128)(2,1)S(1)}, u32[]{:S(2)}, u32[]{:S(2)}) collective-permute-start(bf16[2,256,640]{2,1,0:T(8,128)(2,1)} %get-tuple-element.176.refs_9_), channel_id=1, source_target_pairs={{0,65},{64,0},{1,64},{65,1},{2,67},{66,2},{3,66},{67,3},{4,69},{68... | collective-permute-start | bytes 1966088 | tf_op jit(solution)/shard_map/ppermute | solution.py:394
  127.2 16.7 %attention_back.1 = (bf16[384,1600]{1,0:T(8,128)(2,1)}, f32[384,960]{1,0:T(8,128)}, f32[1,960]{1,0:T(1,128)S(1)}) custom-call(s32[1]{0:T(128)} %bitcast.me_ref, bf16[384,960]{1,0:T(8,128)(2,1)} %get-tuple-element.87.x_ref, f32[2,960]{1,0:T(2,128)S(1)} %reshape.159.gains_ref, f32[384,128]{1,0:T(8,128)S(1)} %copy.44.cos_ref, f32[384,128]{1,0:T(8,128)S(1)} %copy.45.sin_ref, ...), custom_call_target="tpu_custom_call" | custom-call | flops 4152360960 | bytes 16461060 | tf_op jit(solution)/shard_map/attention_back/pallas_call | solution.py:376
  144.1 3.0 %add_convert_fusion.6 = (bf16[2,256,640]{2,1,0:T(8,128)(2,1)}, bf16[2,256,640]{2,1,0:T(8,128)(2,1)}) fusion(bf16[4,256,640]{2,1,0:T(8,128)(2,1)} %collective-permute-done.25, bf16[4,256,640]{2,1,0:T(8,128)(2,1)} %get-tuple-element.107), kind=kLoop, calls=%fused_computation.29 | loop fusion | flops 2621440 | bytes 3932160 | tf_op jit(solution)/shard_map/convert_element_type | solution.py:412
  147.1 6.5 %attention_grad.1 = (bf16[4,256,640]{2,1,0:T(8,128)(2,1)}, bf16[4,256,640]{2,1,0:T(8,128)(2,1)}, bf16[4,256,640]{2,1,0:T(8,128)(2,1)}, bf16[4,256,640]{2,1,0:T(8,128)(2,1)}) custom-call(s32[1]{0:T(128)} %bitcast.me_ref, bf16[960,384]{1,0:T(8,128)(2,1)} %get-tuple-element.101.a_ref, bf16[960,384]{1,0:T(8,128)(2,1)} %get-tuple-element.102.att_ref, ...), custom_call_target="tpu_custom_call" | custom-call | flops 1887436800 | bytes 11386884 | tf_op jit(solution)/shard_map/attention_grad/pallas_call | solution.py:376
  155.5 3.0 %collective-permute-start.32 = (bf16[2,256,640]{2,1,0:T(8,128)(2,1)S(1)}, bf16[2,256,640]{2,1,0:T(8,128)(2,1)S(1)}, u32[]{:S(2)}, u32[]{:S(2)}) collective-permute-start(bf16[2,256,640]{2,1,0:T(8,128)(2,1)S(1)} %copy-done.18), channel_id=1, source_target_pairs={{0,65},{64,0},{1,64},{65,1},{2,67},{66,2},{3,66},{67,3},{4,69},{68... | collective-permute-start | bytes 1966088 | tf_op jit(solution)/shard_map/ppermute | solution.py:394
  158.6 2.0 add_convert_fusion.1
  162.4 1.8 add_convert_fusion
  166.2 7.0 %collective-permute-done.31 = bf16[2,256,640]{2,1,0:T(8,128)(2,1)S(1)} collective-permute-done((bf16[2,256,640]{2,1,0:T(8,128)(2,1)S(1)}, bf16[2,256,640]{2,1,0:T(8,128)(2,1)S(1)}, u32[]{:S(2)}, u32[]{:S(2)}) %collective-permute-start.31) | collective-permute-done | bytes 655392 | tf_op jit(solution)/shard_map/ppermute | solution.py:394
  173.3 3.2 %collective-permute-start.29 = (bf16[2,256,640]{2,1,0:T(8,128)(2,1)S(1)}, bf16[2,256,640]{2,1,0:T(8,128)(2,1)S(1)}, u32[]{:S(2)}, u32[]{:S(2)}) collective-permute-start(bf16[2,256,640]{2,1,0:T(8,128)(2,1)S(1)} %get-tuple-element.173), channel_id=1, source_target_pairs={{0,65},{64,0},{1,64},{65,1},{2,67},{66,2},{3,66},{67,3},{4,69},{68... | collective-permute-start | bytes 1966088 | tf_op jit(solution)/shard_map/ppermute | solution.py:394
  176.5 2.8 collective-permute-start.45
  180.1 5.1 %collective-permute-done.45 = bf16[256,640]{1,0:T(8,128)(2,1)S(1)} collective-permute-done((bf16[256,640]{1,0:T(8,128)(2,1)S(1)}, bf16[256,640]{1,0:T(8,128)(2,1)S(1)}, u32[]{:S(2)}, u32[]{:S(2)}) %collective-permute-start.45) | collective-permute-done | bytes 327712 | tf_op jit(solution)/shard_map/ppermute | solution.py:416
  185.3 3.8 %collective-permute-start.46 = (bf16[512,640]{1,0:T(8,128)(2,1)S(1)}, bf16[512,640]{1,0:T(8,128)(2,1)S(1)}, u32[]{:S(2)}, u32[]{:S(2)}) collective-permute-start(bf16[512,640]{1,0:T(8,128)(2,1)S(1)} %pad_maximum_fusion.4), channel_id=1, source_target_pairs={{0,6},{2,0},{4,2},{6,4},{1,7},{3,1},{5,3},{7,5},{8,14},{10,8},{12,... | collective-permute-start | bytes 1966088 | tf_op jit(solution)/shard_map/ppermute | solution.py:416
  191.1 2.1 collective-permute-start.33
  193.2 2.2 collective-permute-start.35
  195.5 6.1 %collective-permute-done.33 = bf16[256,640]{1,0:T(8,128)(2,1)S(1)} collective-permute-done((bf16[256,640]{1,0:T(8,128)(2,1)S(1)}, bf16[256,640]{1,0:T(8,128)(2,1)S(1)}, u32[]{:S(2)}, u32[]{:S(2)}) %collective-permute-start.33) | collective-permute-done | bytes 327712 | tf_op jit(solution)/shard_map/ppermute | solution.py:416
  203.5 3.2 %collective-permute-start.36 = (bf16[512,640]{1,0:T(8,128)(2,1)}, bf16[512,640]{1,0:T(8,128)(2,1)}, u32[]{:S(2)}, u32[]{:S(2)}) collective-permute-start(bf16[512,640]{1,0:T(8,128)(2,1)} %pad_maximum_fusion.2), channel_id=1, source_target_pairs={{0,24},{8,0},{16,8},{24,16},{1,25},{9,1},{17,9},{25,17},{2,26},{10... | collective-permute-start | bytes 1966088 | tf_op jit(solution)/shard_map/ppermute | solution.py:416
  207.7 3.2 %collective-permute-start.49 = (bf16[64,640]{1,0:T(8,128)(2,1)S(1)}, bf16[64,640]{1,0:T(8,128)(2,1)}, u32[]{:S(2)}, u32[]{:S(2)}) collective-permute-start(bf16[64,640]{1,0:T(8,128)(2,1)S(1)} %get-tuple-element.194), channel_id=1, source_target_pairs={{0,24},{8,0},{16,8},{24,16},{1,25},{9,1},{17,9},{25,17},{2,26},{10... | collective-permute-start | bytes 245768 | tf_op jit(solution)/shard_map/ppermute | solution.py:416
  210.9 9.2 %collective-permute-done.47 = bf16[64,640]{1,0:T(8,128)(2,1)} collective-permute-done((bf16[64,640]{1,0:T(8,128)(2,1)}, bf16[64,640]{1,0:T(8,128)(2,1)}, u32[]{:S(2)}, u32[]{:S(2)}) %collective-permute-start.47) | collective-permute-done | bytes 81952 | tf_op jit(solution)/shard_map/ppermute | solution.py:416
  223.5 1.8 collective-permute-start.37
  225.3 1.7 collective-permute-start.39
  227.1 3.3 %collective-permute-start.50 = (bf16[128,640]{1,0:T(8,128)(2,1)S(1)}, bf16[128,640]{1,0:T(8,128)(2,1)S(1)}, u32[]{:S(2)}, u32[]{:S(2)}) collective-permute-start(bf16[128,640]{1,0:T(8,128)(2,1)S(1)} %pad_maximum_fusion.11), channel_id=1, source_target_pairs={{0,24},{8,0},{16,8},{24,16},{1,25},{9,1},{17,9},{25,17},{2,26},{10... | collective-permute-start | bytes 491528 | tf_op jit(solution)/shard_map/ppermute | solution.py:416
  232.3 1.8 collective-permute-start.40
  234.2 3.1 %collective-permute-done.38 = bf16[128,640]{1,0:T(8,128)(2,1)S(1)} collective-permute-done((bf16[128,640]{1,0:T(8,128)(2,1)S(1)}, bf16[128,640]{1,0:T(8,128)(2,1)S(1)}, u32[]{:S(2)}, u32[]{:S(2)}) %collective-permute-start.38) | collective-permute-done | bytes 163872 | tf_op jit(solution)/shard_map/ppermute | solution.py:416
  239.3 7.1 %collective-permute-done.51 = bf16[2,128,640]{2,1,0:T(8,128)(2,1)S(1)} collective-permute-done((bf16[2,128,640]{2,1,0:T(8,128)(2,1)S(1)}, bf16[2,128,640]{2,1,0:T(8,128)(2,1)S(1)}, u32[]{:S(2)}, u32[]{:S(2)}) %collective-permute-start.51) | collective-permute-done | bytes 327712 | tf_op jit(solution)/shard_map/ppermute | solution.py:591
  251.1 2.1 collective-permute-start.53
  254.5 2.1 collective-permute-start.63
  258.2 3.2 %collective-permute-start.55 = (bf16[64,640]{1,0:T(8,128)(2,1)S(1)}, bf16[64,640]{1,0:T(8,128)(2,1)S(1)}, u32[]{:S(2)}, u32[]{:S(2)}) collective-permute-start(bf16[64,640]{1,0:T(8,128)(2,1)S(1)} %slice.311), channel_id=1, source_target_pairs={{0,6},{2,0},{4,2},{6,4},{1,7},{3,1},{5,3},{7,5},{8,14},{10,8},{12,... | collective-permute-start | bytes 245768 | tf_op jit(solution)/shard_map/ppermute | solution.py:416
  261.6 3.2 %collective-permute-start.65 = (bf16[512,640]{1,0:T(8,128)(2,1)S(1)}, bf16[512,640]{1,0:T(8,128)(2,1)S(1)}, u32[]{:S(2)}, u32[]{:S(2)}) collective-permute-start(bf16[512,640]{1,0:T(8,128)(2,1)S(1)} %constant_dynamic-update-slice_fusion.5.refs_5_), channel_id=1, source_target_pairs={{0,6},{2,0},{4,2},{6,4},{1,7},{3,1},{5,3},{7,5},{8,14},{10,8},{12,... | collective-permute-start | bytes 1966088 | tf_op jit(solution)/shard_map/ppermute | solution.py:416
  266.5 1.8 collective-permute-start.57
  268.2 8.6 %collective-permute-done.64.refs_6_ = bf16[512,640]{1,0:T(8,128)(2,1)S(1)} collective-permute-done((bf16[512,640]{1,0:T(8,128)(2,1)S(1)}, bf16[512,640]{1,0:T(8,128)(2,1)S(1)}, u32[]{:S(2)}, u32[]{:S(2)}) %collective-permute-start.64) | collective-permute-done | bytes 655392 | tf_op jit(solution)/shard_map/ppermute | solution.py:416
  279.3 3.2 %collective-permute-start.67 = (bf16[256,640]{1,0:T(8,128)(2,1)}, bf16[256,640]{1,0:T(8,128)(2,1)S(1)}, u32[]{:S(2)}, u32[]{:S(2)}) collective-permute-start(bf16[256,640]{1,0:T(8,128)(2,1)} %slice.317), channel_id=1, source_target_pairs={{0,6},{2,0},{4,2},{6,4},{1,7},{3,1},{5,3},{7,5},{8,14},{10,8},{12,... | collective-permute-start | bytes 983048 | tf_op jit(solution)/shard_map/ppermute | solution.py:416
  289.0 2.3 copy.50
  293.0 6.4 %place_gradients.1 = (f32[240,960]{1,0:T(8,128)}, f32[320,240]{1,0:T(8,128)}, f32[320,240]{1,0:T(8,128)}, f32[240,960]{1,0:T(8,128)}, f32[8,256]{1,0:T(8,128)S(1...) custom-call(s32[2]{0:T(128)S(1)} %pad_add_fusion.place_ref, ...), custom_call_target="tpu_custom_call" | custom-call | bytes 15081480 | tf_op jit(solution)/shard_map/place_gradients/pallas_call | solution.py:376
  (251 shorter events, 62.7 us)
Async XLA Ops:
  3.8 22.7 %collective-permute-start.9 = (bf16[960,640]{1,0:T(8,128)(2,1)}, bf16[960,640]{1,0:T(8,128)(2,1)}, u32[]{:S(2)}, u32[]{:S(2)}) collective-permute-start(bf16[960,640]{1,0:T(8,128)(2,1)} %bitcast.182), channel_id=1, source_target_pairs={{0,32},{32,0},{1,33},{33,1},{2,34},{34,2},{3,35},{35,3},{4,36},{36... | collective-permute-start | bytes 3686408 | tf_op jit(solution)/shard_map/ppermute | solution.py:389
  3.8 22.7 %collective-permute-start.10 = (bf16[240,2560]{1,0:T(8,128)(2,1)}, bf16[240,2560]{1,0:T(8,128)(2,1)}, u32[]{:S(2)}, u32[]{:S(2)}) collective-permute-start(bf16[240,2560]{1,0:T(8,128)(2,1)} %refs_10_.1), channel_id=1, source_target_pairs={{0,32},{32,0},{1,33},{33,1},{2,34},{34,2},{3,35},{35,3},{4,36},{36... | collective-permute-start | bytes 3686408 | tf_op jit(solution)/shard_map/ppermute | solution.py:389
  4.3 22.2 %collective-permute-start.8 = (bf16[240,2560]{1,0:T(8,128)(2,1)}, bf16[240,2560]{1,0:T(8,128)(2,1)}, u32[]{:S(2)}, u32[]{:S(2)}) collective-permute-start(bf16[240,2560]{1,0:T(8,128)(2,1)} %refs_6_.1), channel_id=1, source_target_pairs={{0,32},{32,0},{1,33},{33,1},{2,34},{34,2},{3,35},{35,3},{4,36},{36... | collective-permute-start | bytes 3686408 | tf_op jit(solution)/shard_map/ppermute | solution.py:389
  6.7 17.7 %collective-permute-start.3 = (bf16[240,1280]{1,0:T(8,128)(2,1)S(1)}, bf16[240,1280]{1,0:T(8,128)(2,1)}, u32[]{:S(2)}, u32[]{:S(2)}) collective-permute-start(bf16[240,1280]{1,0:T(8,128)(2,1)S(1)} %pad_maximum_fusion.5.refs_0_), channel_id=1, source_target_pairs={{0,64},{64,1},{1,65},{65,0},{2,66},{66,3},{3,67},{67,2},{4,68},{68... | collective-permute-start | bytes 1843208 | tf_op jit(solution)/shard_map/ppermute | solution.py:394
  10.2 16.2 %collective-permute-start.6 = (bf16[240,1280]{1,0:T(8,128)(2,1)}, bf16[240,1280]{1,0:T(8,128)(2,1)}, u32[]{:S(2)}, u32[]{:S(2)}) collective-permute-start(bf16[240,1280]{1,0:T(8,128)(2,1)} %pad_maximum_fusion.6.refs_4_), channel_id=1, source_target_pairs={{0,65},{64,0},{1,64},{65,1},{2,67},{66,2},{3,66},{67,3},{4,69},{68... | collective-permute-start | bytes 1843208 | tf_op jit(solution)/shard_map/ppermute | solution.py:394
  26.5 30.1 %collective-permute-start.13 = (bf16[240,2560]{1,0:T(8,128)(2,1)}, bf16[240,2560]{1,0:T(8,128)(2,1)}, u32[]{:S(2)}, u32[]{:S(2)}) collective-permute-start(bf16[240,2560]{1,0:T(8,128)(2,1)} %refs_10_.1), channel_id=1, source_target_pairs={{0,65},{64,0},{1,64},{65,1},{2,67},{66,2},{3,66},{67,3},{4,69},{68... | collective-permute-start | bytes 3686408 | tf_op jit(solution)/shard_map/ppermute | solution.py:394
  29.3 30.5 %collective-permute-start.11 = (bf16[240,2560]{1,0:T(8,128)(2,1)S(1)}, bf16[240,2560]{1,0:T(8,128)(2,1)}, u32[]{:S(2)}, u32[]{:S(2)}) collective-permute-start(bf16[240,2560]{1,0:T(8,128)(2,1)S(1)} %copy-done), channel_id=1, source_target_pairs={{0,64},{64,1},{1,65},{65,0},{2,66},{66,3},{3,67},{67,2},{4,68},{68... | collective-permute-start | bytes 3686408 | tf_op jit(solution)/shard_map/ppermute | solution.py:394
  56.6 7.1 %collective-permute-start.14 = (bf16[240,2560]{1,0:T(8,128)(2,1)}, bf16[240,2560]{1,0:T(8,128)(2,1)S(1)}, u32[]{:S(2)}, u32[]{:S(2)}) collective-permute-start(bf16[240,2560]{1,0:T(8,128)(2,1)} %collective-permute-done.13.refs_6_.refs_12_), channel_id=1, source_target_pairs={{0,32},{32,0},{1,33},{33,1},{2,34},{34,2},{3,35},{35,3},{4,36},{36... | collective-permute-start | bytes 3686408 | tf_op jit(solution)/shard_map/ppermute | solution.py:389
  59.9 17.5 %collective-permute-start.15 = (bf16[480,640]{1,0:T(8,128)(2,1)S(1)}, bf16[480,640]{1,0:T(8,128)(2,1)S(1)}, u32[]{:S(2)}, u32[]{:S(2)}) collective-permute-start(bf16[480,640]{1,0:T(8,128)(2,1)S(1)} %get-tuple-element.181), channel_id=1, source_target_pairs={{0,64},{64,1},{1,65},{65,0},{2,66},{66,3},{3,67},{67,2},{4,68},{68... | collective-permute-start | bytes 1843208 | tf_op jit(solution)/shard_map/ppermute | solution.py:394
  60.0 17.5 %collective-permute-start.16 = (bf16[480,640]{1,0:T(8,128)(2,1)S(1)}, bf16[480,640]{1,0:T(8,128)(2,1)S(1)}, u32[]{:S(2)}, u32[]{:S(2)}) collective-permute-start(bf16[480,640]{1,0:T(8,128)(2,1)S(1)} %get-tuple-element.180), channel_id=1, source_target_pairs={{0,65},{64,0},{1,64},{65,1},{2,67},{66,2},{3,66},{67,3},{4,69},{68... | collective-permute-start | bytes 1843208 | tf_op jit(solution)/shard_map/ppermute | solution.py:394
  83.2 9.6 %collective-permute-start.18 = (bf16[480,640]{1,0:T(8,128)(2,1)S(1)}, bf16[480,640]{1,0:T(8,128)(2,1)S(1)}, u32[]{:S(2)}, u32[]{:S(2)}) collective-permute-start(bf16[480,640]{1,0:T(8,128)(2,1)S(1)} %collective-permute-done.16.refs_1_.refs_3_), channel_id=1, source_target_pairs={{0,32},{32,0},{1,33},{33,1},{2,34},{34,2},{3,35},{35,3},{4,36},{36... | collective-permute-start | bytes 1843208 | tf_op jit(solution)/shard_map/ppermute | solution.py:389
  83.7 9.1 %collective-permute-start.17 = (bf16[480,640]{1,0:T(8,128)(2,1)S(1)}, bf16[480,640]{1,0:T(8,128)(2,1)S(1)}, u32[]{:S(2)}, u32[]{:S(2)}) collective-permute-start(bf16[480,640]{1,0:T(8,128)(2,1)S(1)} %collective-permute-done.15.refs_0_.refs_2_), channel_id=1, source_target_pairs={{0,32},{32,0},{1,33},{33,1},{2,34},{34,2},{3,35},{35,3},{4,36},{36... | collective-permute-start | bytes 1843208 | tf_op jit(solution)/shard_map/ppermute | solution.py:389
  89.1 20.5 %collective-permute-start.20 = (bf16[2,256,640]{2,1,0:T(8,128)(2,1)S(1)}, bf16[2,256,640]{2,1,0:T(8,128)(2,1)S(1)}, u32[]{:S(2)}, u32[]{:S(2)}) collective-permute-start(bf16[2,256,640]{2,1,0:T(8,128)(2,1)S(1)} %get-tuple-element.179.refs_14_), channel_id=1, source_target_pairs={{0,64},{64,1},{1,65},{65,0},{2,66},{66,3},{3,67},{67,2},{4,68},{68... | collective-permute-start | bytes 1966088 | tf_op jit(solution)/shard_map/ppermute | solution.py:394
  89.1 20.4 %collective-permute-start.21 = (bf16[2,256,640]{2,1,0:T(8,128)(2,1)S(1)}, bf16[2,256,640]{2,1,0:T(8,128)(2,1)S(1)}, u32[]{:S(2)}, u32[]{:S(2)}) collective-permute-start(bf16[2,256,640]{2,1,0:T(8,128)(2,1)S(1)} %get-tuple-element.178.refs_15_), channel_id=1, source_target_pairs={{0,65},{64,0},{1,64},{65,1},{2,67},{66,2},{3,66},{67,3},{4,69},{68... | collective-permute-start | bytes 1966088 | tf_op jit(solution)/shard_map/ppermute | solution.py:394
  121.5 22.6 %collective-permute-start.25 = (bf16[4,256,640]{2,1,0:T(8,128)(2,1)}, bf16[4,256,640]{2,1,0:T(8,128)(2,1)}, u32[]{:S(2)}, u32[]{:S(2)}) collective-permute-start(bf16[4,256,640]{2,1,0:T(8,128)(2,1)} %get-tuple-element.108), channel_id=1, source_target_pairs={{0,32},{32,0},{1,33},{33,1},{2,34},{34,2},{3,35},{35,3},{4,36},{36... | collective-permute-start | bytes 3932168 | tf_op jit(solution)/shard_map/ppermute | solution.py:389
  122.5 32.8 %collective-permute-start.41 = (bf16[4,256,640]{2,1,0:T(8,128)(2,1)}, bf16[4,256,640]{2,1,0:T(8,128)(2,1)}, u32[]{:S(2)}, u32[]{:S(2)}) collective-permute-start(bf16[4,256,640]{2,1,0:T(8,128)(2,1)} %get-tuple-element.121), channel_id=1, source_target_pairs={{0,32},{32,0},{1,33},{33,1},{2,34},{34,2},{3,35},{35,3},{4,36},{36... | collective-permute-start | bytes 3932168 | tf_op jit(solution)/shard_map/ppermute | solution.py:389
  124.0 23.1 %collective-permute-start.23 = (bf16[2,256,640]{2,1,0:T(8,128)(2,1)}, bf16[2,256,640]{2,1,0:T(8,128)(2,1)S(1)}, u32[]{:S(2)}, u32[]{:S(2)}) collective-permute-start(bf16[2,256,640]{2,1,0:T(8,128)(2,1)} %get-tuple-element.177.refs_8_), channel_id=1, source_target_pairs={{0,64},{64,1},{1,65},{65,0},{2,66},{66,3},{3,67},{67,2},{4,68},{68... | collective-permute-start | bytes 1966088 | tf_op jit(solution)/shard_map/ppermute | solution.py:394
  124.0 23.1 %collective-permute-start.24 = (bf16[2,256,640]{2,1,0:T(8,128)(2,1)}, bf16[2,256,640]{2,1,0:T(8,128)(2,1)S(1)}, u32[]{:S(2)}, u32[]{:S(2)}) collective-permute-start(bf16[2,256,640]{2,1,0:T(8,128)(2,1)} %get-tuple-element.176.refs_9_), channel_id=1, source_target_pairs={{0,65},{64,0},{1,64},{65,1},{2,67},{66,2},{3,66},{67,3},{4,69},{68... | collective-permute-start | bytes 1966088 | tf_op jit(solution)/shard_map/ppermute | solution.py:394
  153.7 8.7 %collective-permute-start.42 = (bf16[4,256,640]{2,1,0:T(8,128)(2,1)}, bf16[4,256,640]{2,1,0:T(8,128)(2,1)}, u32[]{:S(2)}, u32[]{:S(2)}) collective-permute-start(bf16[4,256,640]{2,1,0:T(8,128)(2,1)} %get-tuple-element.123), channel_id=1, source_target_pairs={{0,32},{32,0},{1,33},{33,1},{2,34},{34,2},{3,35},{35,3},{4,36},{36... | collective-permute-start | bytes 3932168 | tf_op jit(solution)/shard_map/ppermute | solution.py:389
  154.2 22.3 %collective-permute-start.30 = (bf16[4,256,640]{2,1,0:T(8,128)(2,1)}, bf16[4,256,640]{2,1,0:T(8,128)(2,1)S(1)}, u32[]{:S(2)}, u32[]{:S(2)}) collective-permute-start(bf16[4,256,640]{2,1,0:T(8,128)(2,1)} %get-tuple-element.116), channel_id=1, source_target_pairs={{0,32},{32,0},{1,33},{33,1},{2,34},{34,2},{3,35},{35,3},{4,36},{36... | collective-permute-start | bytes 3932168 | tf_op jit(solution)/shard_map/ppermute | solution.py:389
  155.3 17.9 %collective-permute-start.31 = (bf16[2,256,640]{2,1,0:T(8,128)(2,1)S(1)}, bf16[2,256,640]{2,1,0:T(8,128)(2,1)S(1)}, u32[]{:S(2)}, u32[]{:S(2)}) collective-permute-start(bf16[2,256,640]{2,1,0:T(8,128)(2,1)S(1)} %copy-done.19), channel_id=1, source_target_pairs={{0,64},{64,1},{1,65},{65,0},{2,66},{66,3},{3,67},{67,2},{4,68},{68... | collective-permute-start | bytes 1966088 | tf_op jit(solution)/shard_map/ppermute | solution.py:394
  155.5 17.8 %collective-permute-start.32 = (bf16[2,256,640]{2,1,0:T(8,128)(2,1)S(1)}, bf16[2,256,640]{2,1,0:T(8,128)(2,1)S(1)}, u32[]{:S(2)}, u32[]{:S(2)}) collective-permute-start(bf16[2,256,640]{2,1,0:T(8,128)(2,1)S(1)} %copy-done.18), channel_id=1, source_target_pairs={{0,65},{64,0},{1,64},{65,1},{2,67},{66,2},{3,66},{67,3},{4,69},{68... | collective-permute-start | bytes 1966088 | tf_op jit(solution)/shard_map/ppermute | solution.py:394
  160.5 28.5 %collective-permute-start.26 = (bf16[4,256,640]{2,1,0:T(8,128)(2,1)S(1)}, bf16[4,256,640]{2,1,0:T(8,128)(2,1)S(1)}, u32[]{:S(2)}, u32[]{:S(2)}) collective-permute-start(bf16[4,256,640]{2,1,0:T(8,128)(2,1)S(1)} %copy-done.25), channel_id=1, source_target_pairs={{0,32},{32,0},{1,33},{33,1},{2,34},{34,2},{3,35},{35,3},{4,36},{36... | collective-permute-start | bytes 3932168 | tf_op jit(solution)/shard_map/ppermute | solution.py:389
  164.5 15.4 %collective-permute-start.43 = (bf16[256,640]{1,0:T(8,128)(2,1)S(1)}, bf16[256,640]{1,0:T(8,128)(2,1)S(1)}, u32[]{:S(2)}, u32[]{:S(2)}) collective-permute-start(bf16[256,640]{1,0:T(8,128)(2,1)S(1)} %get-tuple-element.196), channel_id=1, source_target_pairs={{0,2},{2,4},{4,6},{6,0},{1,3},{3,5},{5,7},{7,1},{8,10},{10,12},{12... | collective-permute-start | bytes 983048 | tf_op jit(solution)/shard_map/ppermute | solution.py:416
  173.2 17.1 %collective-permute-start.28 = (bf16[2,256,640]{2,1,0:T(8,128)(2,1)S(1)}, bf16[2,256,640]{2,1,0:T(8,128)(2,1)S(1)}, u32[]{:S(2)}, u32[]{:S(2)}) collective-permute-start(bf16[2,256,640]{2,1,0:T(8,128)(2,1)S(1)} %get-tuple-element.172), channel_id=1, source_target_pairs={{0,64},{64,1},{1,65},{65,0},{2,66},{66,3},{3,67},{67,2},{4,68},{68... | collective-permute-start | bytes 1966088 | tf_op jit(solution)/shard_map/ppermute | solution.py:394
  173.3 17.1 %collective-permute-start.29 = (bf16[2,256,640]{2,1,0:T(8,128)(2,1)S(1)}, bf16[2,256,640]{2,1,0:T(8,128)(2,1)S(1)}, u32[]{:S(2)}, u32[]{:S(2)}) collective-permute-start(bf16[2,256,640]{2,1,0:T(8,128)(2,1)S(1)} %get-tuple-element.173), channel_id=1, source_target_pairs={{0,65},{64,0},{1,64},{65,1},{2,67},{66,2},{3,66},{67,3},{4,69},{68... | collective-permute-start | bytes 1966088 | tf_op jit(solution)/shard_map/ppermute | solution.py:394
  176.5 8.7 %collective-permute-start.45 = (bf16[256,640]{1,0:T(8,128)(2,1)S(1)}, bf16[256,640]{1,0:T(8,128)(2,1)S(1)}, u32[]{:S(2)}, u32[]{:S(2)}) collective-permute-start(bf16[256,640]{1,0:T(8,128)(2,1)S(1)} %get-tuple-element.197), channel_id=1, source_target_pairs={{0,6},{2,0},{4,2},{6,4},{1,7},{3,1},{5,3},{7,5},{8,14},{10,8},{12,... | collective-permute-start | bytes 983048 | tf_op jit(solution)/shard_map/ppermute | solution.py:416
  180.0 26.7 %collective-permute-start.44 = (bf16[512,640]{1,0:T(8,128)(2,1)S(1)}, bf16[512,640]{1,0:T(8,128)(2,1)S(1)}, u32[]{:S(2)}, u32[]{:S(2)}) collective-permute-start(bf16[512,640]{1,0:T(8,128)(2,1)S(1)} %pad_maximum_fusion.3), channel_id=1, source_target_pairs={{0,2},{2,4},{4,6},{6,0},{1,3},{3,5},{5,7},{7,1},{8,10},{10,12},{12... | collective-permute-start | bytes 1966088 | tf_op jit(solution)/shard_map/ppermute | solution.py:416
  185.3 21.4 %collective-permute-start.46 = (bf16[512,640]{1,0:T(8,128)(2,1)S(1)}, bf16[512,640]{1,0:T(8,128)(2,1)S(1)}, u32[]{:S(2)}, u32[]{:S(2)}) collective-permute-start(bf16[512,640]{1,0:T(8,128)(2,1)S(1)} %pad_maximum_fusion.4), channel_id=1, source_target_pairs={{0,6},{2,0},{4,2},{6,4},{1,7},{3,1},{5,3},{7,5},{8,14},{10,8},{12,... | collective-permute-start | bytes 1966088 | tf_op jit(solution)/shard_map/ppermute | solution.py:416
  191.1 10.4 %collective-permute-start.33 = (bf16[256,640]{1,0:T(8,128)(2,1)S(1)}, bf16[256,640]{1,0:T(8,128)(2,1)S(1)}, u32[]{:S(2)}, u32[]{:S(2)}) collective-permute-start(bf16[256,640]{1,0:T(8,128)(2,1)S(1)} %get-tuple-element.188), channel_id=1, source_target_pairs={{0,8},{8,16},{16,24},{24,0},{1,9},{9,17},{17,25},{25,1},{2,10},{10... | collective-permute-start | bytes 983048 | tf_op jit(solution)/shard_map/ppermute | solution.py:416
  193.2 9.3 %collective-permute-start.35 = (bf16[256,640]{1,0:T(8,128)(2,1)S(1)}, bf16[256,640]{1,0:T(8,128)(2,1)S(1)}, u32[]{:S(2)}, u32[]{:S(2)}) collective-permute-start(bf16[256,640]{1,0:T(8,128)(2,1)S(1)} %get-tuple-element.189), channel_id=1, source_target_pairs={{0,24},{8,0},{16,8},{24,16},{1,25},{9,1},{17,9},{25,17},{2,26},{10... | collective-permute-start | bytes 983048 | tf_op jit(solution)/shard_map/ppermute | solution.py:416
  202.5 19.4 %collective-permute-start.34 = (bf16[512,640]{1,0:T(8,128)(2,1)}, bf16[512,640]{1,0:T(8,128)(2,1)}, u32[]{:S(2)}, u32[]{:S(2)}) collective-permute-start(bf16[512,640]{1,0:T(8,128)(2,1)} %pad_maximum_fusion.1), channel_id=1, source_target_pairs={{0,8},{8,16},{16,24},{24,0},{1,9},{9,17},{17,25},{25,1},{2,10},{10... | collective-permute-start | bytes 1966088 | tf_op jit(solution)/shard_map/ppermute | solution.py:416
  203.5 18.4 %collective-permute-start.36 = (bf16[512,640]{1,0:T(8,128)(2,1)}, bf16[512,640]{1,0:T(8,128)(2,1)}, u32[]{:S(2)}, u32[]{:S(2)}) collective-permute-start(bf16[512,640]{1,0:T(8,128)(2,1)} %pad_maximum_fusion.2), channel_id=1, source_target_pairs={{0,24},{8,0},{16,8},{24,16},{1,25},{9,1},{17,9},{25,17},{2,26},{10... | collective-permute-start | bytes 1966088 | tf_op jit(solution)/shard_map/ppermute | solution.py:416
  207.7 12.5 %collective-permute-start.47 = (bf16[64,640]{1,0:T(8,128)(2,1)}, bf16[64,640]{1,0:T(8,128)(2,1)}, u32[]{:S(2)}, u32[]{:S(2)}) collective-permute-start(bf16[64,640]{1,0:T(8,128)(2,1)} %get-tuple-element.192), channel_id=1, source_target_pairs={{0,8},{8,16},{16,24},{24,0},{1,9},{9,17},{17,25},{25,1},{2,10},{10... | collective-permute-start | bytes 245768 | tf_op jit(solution)/shard_map/ppermute | solution.py:416
  207.7 12.6 %collective-permute-start.49 = (bf16[64,640]{1,0:T(8,128)(2,1)S(1)}, bf16[64,640]{1,0:T(8,128)(2,1)}, u32[]{:S(2)}, u32[]{:S(2)}) collective-permute-start(bf16[64,640]{1,0:T(8,128)(2,1)S(1)} %get-tuple-element.194), channel_id=1, source_target_pairs={{0,24},{8,0},{16,8},{24,16},{1,25},{9,1},{17,9},{25,17},{2,26},{10... | collective-permute-start | bytes 245768 | tf_op jit(solution)/shard_map/ppermute | solution.py:416
  221.3 12.8 %collective-permute-start.48 = (bf16[128,640]{1,0:T(8,128)(2,1)S(1)}, bf16[128,640]{1,0:T(8,128)(2,1)S(1)}, u32[]{:S(2)}, u32[]{:S(2)}) collective-permute-start(bf16[128,640]{1,0:T(8,128)(2,1)S(1)} %pad_maximum_fusion.10), channel_id=1, source_target_pairs={{0,8},{8,16},{16,24},{24,0},{1,9},{9,17},{17,25},{25,1},{2,10},{10... | collective-permute-start | bytes 491528 | tf_op jit(solution)/shard_map/ppermute | solution.py:416
  237.8 8.7 %collective-permute-start.51 = (bf16[2,128,640]{2,1,0:T(8,128)(2,1)S(1)}, bf16[2,128,640]{2,1,0:T(8,128)(2,1)S(1)}, u32[]{:S(2)}, u32[]{:S(2)}) collective-permute-start(bf16[2,128,640]{2,1,0:T(8,128)(2,1)S(1)} %pad_maximum_fusion.7), channel_id=1, source_target_pairs={{0,1},{1,0},{2,3},{3,2},{4,5},{5,4},{6,7},{7,6},{8,9},{9,8},{10,11... | collective-permute-start | bytes 983048 | tf_op jit(solution)/shard_map/ppermute | solution.py:591
  249.9 7.9 %collective-permute-start.52 = (bf16[128,640]{1,0:T(8,128)(2,1)S(1)}, bf16[128,640]{1,0:T(8,128)(2,1)S(1)}, u32[]{:S(2)}, u32[]{:S(2)}) collective-permute-start(bf16[128,640]{1,0:T(8,128)(2,1)S(1)} %get-tuple-element.199), channel_id=1, source_target_pairs={{0,2},{2,4},{4,6},{6,0},{1,3},{3,5},{5,7},{7,1},{8,10},{10,12},{12... | collective-permute-start | bytes 491528 | tf_op jit(solution)/shard_map/ppermute | solution.py:416
  251.1 7.1 %collective-permute-start.53 = (bf16[128,640]{1,0:T(8,128)(2,1)S(1)}, bf16[128,640]{1,0:T(8,128)(2,1)S(1)}, u32[]{:S(2)}, u32[]{:S(2)}) collective-permute-start(bf16[128,640]{1,0:T(8,128)(2,1)S(1)} %get-tuple-element.199), channel_id=1, source_target_pairs={{0,6},{2,0},{4,2},{6,4},{1,7},{3,1},{5,3},{7,5},{8,14},{10,8},{12,... | collective-permute-start | bytes 491528 | tf_op jit(solution)/shard_map/ppermute | solution.py:416
  253.2 8.3 %collective-permute-start.62 = (bf16[64,640]{1,0:T(8,128)(2,1)S(1)}, bf16[64,640]{1,0:T(8,128)(2,1)S(1)}, u32[]{:S(2)}, u32[]{:S(2)}) collective-permute-start(bf16[64,640]{1,0:T(8,128)(2,1)S(1)} %slice.314), channel_id=1, source_target_pairs={{0,8},{8,16},{16,24},{24,0},{1,9},{9,17},{17,25},{25,1},{2,10},{10... | collective-permute-start | bytes 245768 | tf_op jit(solution)/shard_map/ppermute | solution.py:416
  261.6 15.3 %collective-permute-start.64 = (bf16[512,640]{1,0:T(8,128)(2,1)S(1)}, bf16[512,640]{1,0:T(8,128)(2,1)S(1)}, u32[]{:S(2)}, u32[]{:S(2)}) collective-permute-start(bf16[512,640]{1,0:T(8,128)(2,1)S(1)} %constant_dynamic-update-slice_fusion.5.refs_5_), channel_id=1, source_target_pairs={{0,2},{2,4},{4,6},{6,0},{1,3},{3,5},{5,7},{7,1},{8,10},{10,12},{12... | collective-permute-start | bytes 1966088 | tf_op jit(solution)/shard_map/ppermute | solution.py:416
  261.6 16.8 %collective-permute-start.65 = (bf16[512,640]{1,0:T(8,128)(2,1)S(1)}, bf16[512,640]{1,0:T(8,128)(2,1)S(1)}, u32[]{:S(2)}, u32[]{:S(2)}) collective-permute-start(bf16[512,640]{1,0:T(8,128)(2,1)S(1)} %constant_dynamic-update-slice_fusion.5.refs_5_), channel_id=1, source_target_pairs={{0,6},{2,0},{4,2},{6,4},{1,7},{3,1},{5,3},{7,5},{8,14},{10,8},{12,... | collective-permute-start | bytes 1966088 | tf_op jit(solution)/shard_map/ppermute | solution.py:416
  264.9 17.6 %collective-permute-start.56 = (bf16[512,640]{1,0:T(8,128)(2,1)S(1)}, bf16[512,640]{1,0:T(8,128)(2,1)S(1)}, u32[]{:S(2)}, u32[]{:S(2)}) collective-permute-start(bf16[512,640]{1,0:T(8,128)(2,1)S(1)} %constant_dynamic-update-slice_fusion.refs_0_), channel_id=1, source_target_pairs={{0,8},{8,16},{16,24},{24,0},{1,9},{9,17},{17,25},{25,1},{2,10},{10... | collective-permute-start | bytes 1966088 | tf_op jit(solution)/shard_map/ppermute | solution.py:416
  266.5 18.4 %collective-permute-start.57 = (bf16[512,640]{1,0:T(8,128)(2,1)S(1)}, bf16[512,640]{1,0:T(8,128)(2,1)S(1)}, u32[]{:S(2)}, u32[]{:S(2)}) collective-permute-start(bf16[512,640]{1,0:T(8,128)(2,1)S(1)} %constant_dynamic-update-slice_fusion.refs_0_), channel_id=1, source_target_pairs={{0,24},{8,0},{16,8},{24,16},{1,25},{9,1},{17,9},{25,17},{2,26},{10... | collective-permute-start | bytes 1966088 | tf_op jit(solution)/shard_map/ppermute | solution.py:416
  278.4 12.9 %collective-permute-start.66 = (bf16[256,640]{1,0:T(8,128)(2,1)}, bf16[256,640]{1,0:T(8,128)(2,1)S(1)}, u32[]{:S(2)}, u32[]{:S(2)}) collective-permute-start(bf16[256,640]{1,0:T(8,128)(2,1)} %slice.316), channel_id=1, source_target_pairs={{0,2},{2,4},{4,6},{6,0},{1,3},{3,5},{5,7},{7,1},{8,10},{10,12},{12... | collective-permute-start | bytes 983048 | tf_op jit(solution)/shard_map/ppermute | solution.py:416
  279.3 12.1 %collective-permute-start.67 = (bf16[256,640]{1,0:T(8,128)(2,1)}, bf16[256,640]{1,0:T(8,128)(2,1)S(1)}, u32[]{:S(2)}, u32[]{:S(2)}) collective-permute-start(bf16[256,640]{1,0:T(8,128)(2,1)} %slice.317), channel_id=1, source_target_pairs={{0,6},{2,0},{4,2},{6,4},{1,7},{3,1},{5,3},{7,5},{8,14},{10,8},{12,... | collective-permute-start | bytes 983048 | tf_op jit(solution)/shard_map/ppermute | solution.py:416
  283.3 8.5 %collective-permute-start.58 = (bf16[256,640]{1,0:T(8,128)(2,1)}, bf16[256,640]{1,0:T(8,128)(2,1)S(1)}, u32[]{:S(2)}, u32[]{:S(2)}) collective-permute-start(bf16[256,640]{1,0:T(8,128)(2,1)} %slice.312), channel_id=1, source_target_pairs={{0,8},{8,16},{16,24},{24,0},{1,9},{9,17},{17,25},{25,1},{2,10},{10... | collective-permute-start | bytes 983048 | tf_op jit(solution)/shard_map/ppermute | solution.py:416
  285.7 7.3 %collective-permute-start.59 = (bf16[256,640]{1,0:T(8,128)(2,1)}, bf16[256,640]{1,0:T(8,128)(2,1)S(1)}, u32[]{:S(2)}, u32[]{:S(2)}) collective-permute-start(bf16[256,640]{1,0:T(8,128)(2,1)} %slice.313), channel_id=1, source_target_pairs={{0,24},{8,0},{16,8},{24,16},{1,25},{9,1},{17,9},{25,17},{2,26},{10... | collective-permute-start | bytes 983048 | tf_op jit(solution)/shard_map/ppermute | solution.py:416
  (51 other events, 382.8 us)
